TPU v7x, 32 devices: a whole 2x2x4 slice. The times are simulated.
32 devices in a mesh: dp: 16 (over z, y, x), seq: 2 (over core).
Axes of the slice: x: 2, y: 2, z: 4, core: 2. Of those that a mesh axis runs over, the one named last changes fastest.
Arguments:
- hidden: bfloat16 [48, 512, 768], P('dp', 'seq'), may hold values from -6 to 6
- span_mask: int32 [48, 512], P('dp', 'seq'), may hold values 0 or 1
- replace_kind: int32 [48, 512], P('dp', 'seq'), may hold values from 0 to 9
- replace_from: int32 [48, 512], P('dp', 'seq'), may hold values from 0 to 255
- weights: float32 [9216, 768], P('dp'), may hold values from -0.48549177 to 0.48549177
- vectors: float32 [13, 768], P(None, 'dp'), may hold values from -4 to 4
- weight_first: float32 [9216, 768], P('dp'), may hold values from -0.00061035156 to 0.00061035156
- weight_second: float32 [9216, 768], P('dp'), may hold values from 7.054304e-11 to 1.1286886e-09
- vector_first: float32 [13, 768], P(None, 'dp'), may hold values from -0.00061035156 to 0.00061035156
- vector_second: float32 [13, 768], P(None, 'dp'), may hold values from 7.054304e-11 to 1.1286886e-09
- cotangent: bfloat16 [48, 512, 768], P('dp', 'seq'), may hold values from -6 to 6
Outputs:
- layer_out: float32 [48, 512, 768], P('dp', 'seq')
- input_grad: float32 [48, 512, 768], P('dp', 'seq')
- grad_norm: float32 [], replicated
- weights_new: float32 [9216, 768], P('dp')
- weight_first_new: float32 [9216, 768], P('dp')
- weight_second_new: float32 [9216, 768], P('dp')
- vectors_new: float32 [13, 768], P(None, 'dp')
- vector_first_new: float32 [13, 768], P(None, 'dp')
- vector_second_new: float32 [13, 768], P(None, 'dp')
- weights_low: bfloat16 [9216, 768], P('dp')
- vectors_low: bfloat16 [13, 768], P(None, 'dp')
All inputs are finite; a program needn't handle non-finite values. No bound on the sum of `span_mask` on one device may be relied on, other than what follows from the above.
Results may differ from a plain program's by a relative error of at most 0.015.
The roundings to bfloat16 on the way count: a program that leaves them out, or rounds other values in their place, can miss the bound.
Values may be sent and summed in bfloat16 or wider, within the bound.
No kernel may reach another device: no remote copies, remote signals or barrier semaphores. Data moves between devices by JAX's collectives and lax.ppermute only.
A program may use at most 192 MiB of HBM per device.

v0:
```python
import jax
import jax.numpy as jnp
from jax import lax
from jax.sharding import PartitionSpec as P

D = 768
HEADS = 12
HEAD_DIM = 64
FF = 3072
STEP = 10


ln_eps = 1e-12
beta_one = 0.9
beta_two = 0.999
adam_eps = 1e-08
learn_rate = 0.05
vector_rate = 0.3
decay_rate = 0.01


def split_matrices(stacked):
    return (
        stacked[: 3 * D],
        stacked[3 * D : 4 * D],
        stacked[4 * D : 4 * D + FF],
        stacked[4 * D + FF :],
    )


def layer_norm(values, gain, shift):
    center = values - jnp.mean(values, axis=-1, keepdims=True)
    inv_std = lax.rsqrt(jnp.mean(center * center, axis=-1, keepdims=True) + ln_eps)
    normed = center * inv_std
    return (normed * gain + shift, normed, inv_std)


def norm_backward(upstream, normed, inv_std, gain):
    scaled = upstream * gain
    return inv_std * (
        scaled
        - jnp.mean(scaled, axis=-1, keepdims=True)
        - normed * jnp.mean(scaled * normed, axis=-1, keepdims=True)
    )


def corrupt(initial, mask_row, span_mask, replace_kind, source):
    picked = jax.vmap(lambda seq_rows, where_from: seq_rows[where_from])(initial, source)
    chosen = span_mask == 1
    masked = (chosen & (replace_kind < 8))[..., None]
    swapped = (chosen & (replace_kind == 8))[..., None]
    return jnp.where(masked, mask_row, jnp.where(swapped, picked, initial))


def gelu_exact(points):
    return jax.nn.gelu(points, approximate=False)


def head_split(block):
    return block.reshape(block.shape[0], HEADS, HEAD_DIM)


def score_block(query_heads, key_heads):
    return jnp.einsum(
        "qhd,khd->hqk", query_heads, key_heads, preferred_element_type=jnp.float32
    ) * HEAD_DIM ** (-0.5)


def attend_forward(operands):
    queries, keys_all, values_all = operands
    query_heads = head_split(queries)
    scores = score_block(query_heads, head_split(keys_all))
    row_max = jnp.max(scores, axis=-1, keepdims=True)
    exponents = jnp.exp(scores - row_max)
    row_total = jnp.sum(exponents, axis=-1, keepdims=True)
    probabilities = exponents / row_total
    attended = jnp.einsum(
        "hqk,khd->qhd",
        probabilities.astype(jnp.bfloat16),
        head_split(values_all),
        preferred_element_type=jnp.float32,
    )
    return (attended.reshape(queries.shape[0], D), (row_max + jnp.log(row_total))[..., 0])


def attend_backward(operands):
    queries, keys_all, values_all, grad_attended, log_total, row_delta = operands
    query_heads = head_split(queries)
    key_heads = head_split(keys_all)
    grad_heads = head_split(grad_attended)
    probabilities = jnp.exp(score_block(query_heads, key_heads) - log_total[..., None])
    grad_probs = jnp.einsum(
        "qhd,khd->hqk", grad_heads, head_split(values_all), preferred_element_type=jnp.float32
    )
    grad_scores = (probabilities * (grad_probs - row_delta[..., None])).astype(jnp.bfloat16)
    grad_queries = jnp.einsum(
        "hqk,khd->qhd", grad_scores, key_heads, preferred_element_type=jnp.float32
    ) * HEAD_DIM ** (-0.5)
    grad_keys = jnp.einsum(
        "hqk,qhd->khd", grad_scores, query_heads, preferred_element_type=jnp.float32
    ) * HEAD_DIM ** (-0.5)
    grad_values = jnp.einsum(
        "hqk,qhd->khd",
        probabilities.astype(jnp.bfloat16),
        grad_heads,
        preferred_element_type=jnp.float32,
    )
    key_count = keys_all.shape[0]
    return (
        grad_queries.reshape(queries.shape[0], D),
        grad_keys.reshape(key_count, D),
        grad_values.reshape(key_count, D),
    )


def adam_step(master, first_old, second, gradient, decay_on, step_rate):
    first_new = beta_one * first_old + (1.0 - beta_one) * gradient
    second_new = beta_two * second + (1.0 - beta_two) * gradient * gradient
    fix_one = 1.0 - beta_one**STEP
    fix_two = 1.0 - beta_two**STEP
    update = first_new / fix_one / (jnp.sqrt(second_new / fix_two) + adam_eps)
    return (master - step_rate * (update + decay_on * master), first_new, second_new)


def shards(
    hidden,
    span_mask,
    replace_kind,
    replace_from,
    weights,
    vectors,
    weight_first,
    weight_second,
    vector_first,
    vector_second,
    cotangent,
):
    seq_count = hidden.shape[0]
    half_len = hidden.shape[1]
    row_count = seq_count * half_len
    low_weights = weights.astype(jnp.bfloat16)
    low_vectors = vectors.astype(jnp.bfloat16)
    full_w, full_v = (
        lax.all_gather(low_weights, "dp", axis=0, tiled=True),
        lax.all_gather(low_vectors, "dp", axis=1, tiled=True),
    )
    w_qkv, w_out, w_in, w_back = split_matrices(full_w)
    params = full_v.astype(jnp.float32)
    initial = hidden.astype(jnp.float32)

    def corrupt_local(values, mask_row):
        return corrupt(values, mask_row, span_mask, replace_kind, replace_from)

    inputs, corrupt_pull = jax.vjp(corrupt_local, initial, params[8])
    input_rows = inputs.reshape(row_count, D)
    input_low = input_rows.astype(jnp.bfloat16)
    bias_qkv = jnp.concatenate([params[0], jnp.zeros((D,), jnp.float32), params[1]])
    projected = (
        jnp.einsum("rd,ed->re", input_low, w_qkv, preferred_element_type=jnp.float32) + bias_qkv
    ).astype(jnp.bfloat16)
    queries = projected[:, :D].reshape(seq_count, half_len, D)
    keys_local = projected[:, D : 2 * D].reshape(seq_count, half_len, D)
    values_local = projected[:, 2 * D :].reshape(seq_count, half_len, D)
    keys_all, values_all = (
        lax.all_gather(keys_local, "seq", axis=1, tiled=True),
        lax.all_gather(values_local, "seq", axis=1, tiled=True),
    )
    attended, log_total = lax.map(attend_forward, (queries, keys_all, values_all))
    attended_rows = attended.reshape(row_count, D)
    attended_low = attended_rows.astype(jnp.bfloat16)
    branch = (
        jnp.einsum("rd,ed->re", attended_low, w_out, preferred_element_type=jnp.float32) + params[2]
    )
    hidden_one, normed_one, inv_one = layer_norm(input_rows + branch, params[3], params[4])
    hidden_low = hidden_one.astype(jnp.bfloat16)
    preact = jnp.einsum("rd,fd->rf", hidden_low, w_in, preferred_element_type=jnp.float32) + params[
        9:
    ].reshape(FF)
    activation, gelu_pull = jax.vjp(gelu_exact, preact)
    gelu_low = activation.astype(jnp.bfloat16)
    feed_out = (
        jnp.einsum("rf,fd->rd", gelu_low, w_back, preferred_element_type=jnp.float32) + params[5]
    )
    layer_out, normed_two, inv_two = layer_norm(hidden_one + feed_out, params[6], params[7])
    back_w, back_v = (
        lax.all_gather(low_weights, "dp", axis=0, tiled=True),
        lax.all_gather(low_vectors, "dp", axis=1, tiled=True),
    )
    back_qkv, back_out, back_in, back_down = split_matrices(back_w)
    vector_vals = back_v.astype(jnp.float32)
    grad_out = cotangent.astype(jnp.float32).reshape(row_count, D)
    grad_two = norm_backward(grad_out, normed_two, inv_two, vector_vals[6])
    grad_feed = grad_two.astype(jnp.bfloat16)
    grad_gelu = jnp.einsum("rd,fd->rf", grad_feed, back_down, preferred_element_type=jnp.float32)
    grad_preact = gelu_pull(grad_gelu)[0].astype(jnp.bfloat16)
    grad_hidden = grad_two + jnp.einsum(
        "rf,fd->rd", grad_preact, back_in, preferred_element_type=jnp.float32
    )
    grad_one = norm_backward(grad_hidden, normed_one, inv_one, vector_vals[3])
    grad_branch = grad_one.astype(jnp.bfloat16)
    grad_attended = jnp.einsum(
        "re,ed->rd", grad_branch, back_out, preferred_element_type=jnp.float32
    ).astype(jnp.bfloat16)
    row_delta = (grad_attended.astype(jnp.float32) * attended_rows).reshape(
        seq_count, half_len, HEADS, HEAD_DIM
    )
    row_delta = jnp.sum(row_delta, axis=-1).transpose(0, 2, 1)
    keys_back, values_back = (
        lax.all_gather(keys_local, "seq", axis=1, tiled=True),
        lax.all_gather(values_local, "seq", axis=1, tiled=True),
    )
    grad_queries, grad_keys_all, grad_values_all = lax.map(
        attend_backward,
        (
            queries,
            keys_back,
            values_back,
            grad_attended.reshape(seq_count, half_len, D),
            log_total,
            row_delta,
        ),
    )
    grad_keys, grad_values = (
        lax.psum_scatter(
            grad_keys_all.astype(jnp.bfloat16), "seq", scatter_dimension=1, tiled=True
        ).astype(jnp.float32),
        lax.psum_scatter(
            grad_values_all.astype(jnp.bfloat16), "seq", scatter_dimension=1, tiled=True
        ).astype(jnp.float32),
    )
    grad_proj = (
        jnp.concatenate([grad_queries, grad_keys, grad_values], axis=-1)
        .reshape(row_count, 3 * D)
        .astype(jnp.bfloat16)
    )
    grad_inputs = grad_one + jnp.einsum(
        "re,ed->rd", grad_proj, back_qkv, preferred_element_type=jnp.float32
    )
    input_grad, grad_mask = corrupt_pull(grad_inputs.reshape(seq_count, half_len, D))
    grad_qkv_w = jnp.einsum("re,rd->ed", grad_proj, input_low, preferred_element_type=jnp.float32)
    grad_out_w = jnp.einsum(
        "re,rd->ed", grad_branch, attended_low, preferred_element_type=jnp.float32
    )
    grad_in_w = jnp.einsum("rf,rd->fd", grad_preact, hidden_low, preferred_element_type=jnp.float32)
    grad_down_w = jnp.einsum("rf,rd->fd", gelu_low, grad_feed, preferred_element_type=jnp.float32)
    flat_grad = jnp.concatenate([grad_qkv_w, grad_out_w, grad_in_w, grad_down_w], axis=0)
    proj_sums = jnp.sum(grad_proj.astype(jnp.float32), axis=0)
    vector_rows = jnp.stack(
        [
            proj_sums[:D],
            proj_sums[2 * D :],
            jnp.sum(grad_branch.astype(jnp.float32), axis=0),
            jnp.sum(grad_hidden * normed_one, axis=0),
            jnp.sum(grad_hidden, axis=0),
            jnp.sum(grad_feed.astype(jnp.float32), axis=0),
            jnp.sum(grad_out * normed_two, axis=0),
            jnp.sum(grad_out, axis=0),
            grad_mask,
        ]
    )
    bias_rows = jnp.sum(grad_preact.astype(jnp.float32), axis=0).reshape(FF // D, D)
    vector_grad = jnp.concatenate([vector_rows, bias_rows], axis=0)
    shard_w, shard_v = (
        lax.psum_scatter(flat_grad, "dp", scatter_dimension=0, tiled=True),
        lax.psum_scatter(vector_grad, "dp", scatter_dimension=1, tiled=True),
    )
    shard_w, shard_v = (
        lax.psum(shard_w.astype(jnp.bfloat16), "seq").astype(jnp.float32),
        lax.psum(shard_v.astype(jnp.bfloat16), "seq").astype(jnp.float32),
    )
    squares = lax.psum(jnp.sum(shard_w * shard_w) + jnp.sum(shard_v * shard_v), "dp")
    grad_norm = jnp.sqrt(squares)
    clip = 1.0 / jnp.maximum(grad_norm, 1.0)
    weights_new, weight_first_new, weight_second_new = adam_step(
        weights, weight_first, weight_second, shard_w * clip, decay_rate, learn_rate
    )
    vectors_new, vector_first_new, vector_second_new = adam_step(
        vectors, vector_first, vector_second, shard_v * clip, 0.0, vector_rate
    )
    return (
        layer_out.reshape(seq_count, half_len, D),
        input_grad,
        grad_norm,
        weights_new,
        weight_first_new,
        weight_second_new,
        vectors_new,
        vector_first_new,
        vector_second_new,
        weights_new.astype(jnp.bfloat16),
        vectors_new.astype(jnp.bfloat16),
    )


def solution(mesh):
    in_specs = (
        P("dp", "seq", None),
        P("dp", "seq"),
        P("dp", "seq"),
        P("dp", "seq"),
        P("dp", None),
        P(None, "dp"),
        P("dp", None),
        P("dp", None),
        P(None, "dp"),
        P(None, "dp"),
        P("dp", "seq", None),
    )
    out_specs = (
        P("dp", "seq", None),
        P("dp", "seq", None),
        P(),
        P("dp", None),
        P("dp", None),
        P("dp", None),
        P(None, "dp"),
        P(None, "dp"),
        P(None, "dp"),
        P("dp", None),
        P(None, "dp"),
    )
    return jax.shard_map(shards, mesh=mesh, in_specs=in_specs, out_specs=out_specs, check_vma=False)
```

profile of v0, /device:TPU:0, one launch (start us, length us, event | category | flops | bytes accessed | tf_op | source)
XLA Modules:
  0.0 1115.0 jit_solution(16963355369262875344)
XLA Ops:
  7.2 2.6 convert_element_type.113
  9.9 43.3 %all-gather = bf16[16,48,13]{1,2,0:T(8,128)(2,1)S(1)} all-gather(bf16[1,48,13]{1,2,0:T(8,128)(2,1)S(1)} %convert_bitcast_fusion), channel_id=1, replica_groups=mesh['dp'=16,'seq'=2] {'dp'}, dimensions={0}, use_global_device_ids=true | all-gather | bytes 21216 | tf_op jit(solution)/shard_map/all_gather | solution.py:145
  54.8 8.9 gather_fusion
  63.7 1.8 slice_reduce_fusion.1
  66.2 2.1 select_select_fusion
  69.8 111.6 %all-gather.5.cloned.1.call-done = bf16[9216,768]{1,0:T(8,128)(2,1)} async-done(((bf16[576,768]{1,0:T(8,128)(2,1)}), bf16[9216,768]{1,0:T(8,128)(2,1)}) %all-gather.5.cloned.1.call-update) | async-done | bytes 14155792 | tf_op jit(solution)/shard_map/all_gather | solution.py:144
  181.4 5.2 add_convert_fusion.1
  187.8 1.4 copy.54
  189.3 1.5 copy.55
  192.9 1.6 copy.57
  194.6 3.7 all-gather.7.cloned.1.call-done
  198.3 14.0 %all-gather.9.cloned.1.call-done = bf16[3,512,768]{1,2,0:T(8,128)(2,1)} async-done(((bf16[3,256,768]{1,2,0:T(8,128)(2,1)}), bf16[3,512,768]{1,2,0:T(8,128)(2,1)}) %all-gather.9.cloned.1.call-update) | async-done | bytes 2359312 | tf_op jit(solution)/shard_map/all_gather | solution.py:165
  212.3 25.3 %while.28 = (s32[]{:T(128)}, f32[3,256,768]{2,1,0:T(8,128)}, f32[3,12,256]{2,1,0:T(8,128)S(1)}, bf16[3,512,768]{1,2,0:T(8,128)(2,1)}, bf16[3,256,768]{1,2,0:T(8,128)(2,1)S(1)}, /*index=5*/bf16[3,512,768]{1,2,0:T(8,128)(2,1)}) while((s32[]{:T(128)}, f32[3,256,768]{2,1,0:T(8,128)}, f32[3,12,256]{2,1,0:T(8,128)S(1)}, ...), condition=%wide.region_3.4_spmd.clone, body=%wide.region_0.3_spmd.sunk.clone | while | flops 416805888 | bytes 28815452 | solution.py:168
  212.3 1.5 constant_dynamic-slice_fusion.22
  214.9 1.6 fusion.140
  216.5 3.0 fusion.141
  220.7 1.5 constant_dynamic-slice_fusion.22
  223.4 1.6 fusion.140
  225.0 3.0 fusion.141
  229.2 1.5 constant_dynamic-slice_fusion.22
  231.8 1.6 fusion.140
  233.4 3.0 fusion.141
  237.7 1.9 bitcast_convert_fusion
  240.0 2.5 fusion.79
  243.2 28.0 %multiply_convert_fusion.1 = (bf16[768,3072]{1,0:T(8,128)(2,1)S(1)}, f32[768,3072]{1,0:T(8,128)}, f32[768,3072]{1,0:T(8,128)}) fusion(f32[3072]{0:T(1024)S(1)} %add.175, bf16[9216,768]{1,0:T(8,128)(2,1)} %all-gather.5.cloned.1.call-done, f32[768,768]{1,0:T(8,128)S(1)} %get-tuple-element.251, f32[768]{0:T(1024)S(1)} %copy-done.40, ...), kind=kOutput, calls=%fused_computation.37 | convolution fusion | flops 3782541312 | bytes 30695424 | tf_op jit(solution)/shard_map/rd,fd->rf/dot_general | solution.py:176
  271.3 8.1 fusion.80
  280.7 1.5 fusion.34
  282.2 2.9 convert_reduce_fusion.3
  285.2 14.6 %convert_reduce_fusion = (f32[3072]{0:T(1024)}, bf16[768,3072]{1,0:T(8,128)(2,1)}) fusion(f32[768,3072]{1,0:T(8,128)} %get-tuple-element.231, bf16[9216,768]{1,0:T(8,128)(2,1)} %all-gather.5.cloned.1.call-done, f32[768,768]{1,0:T(8,128)S(1)} %get-tuple-element.225, f32[768,3072]{1,0:T(8,128)} %get-tuple-element.252, f32[3072]{0:T(1024)S(1)} %add.175), kind=kOutput, calls=%fused_computation.35 | convolution fusion | flops 3664573440 | bytes 30695424 | tf_op jit(solution)/shard_map/rd,fd->rf/dot_general | solution.py:194
  299.8 8.3 multiply_reduce_fusion.1
  309.7 4.2 bitcast_multiply_fusion.2
  313.9 3.1 copy.59
  317.0 4.7 reshape.186
  321.7 2.3 reduce_sum.198
  324.0 51.2 %while.29 = (s32[]{:T(128)}, bf16[3,256,768]{1,2,0:T(8,128)(2,1)}, bf16[3,512,768]{1,2,0:T(8,128)(2,1)}, bf16[3,512,768]{1,2,0:T(8,128)(2,1)}, bf16[3,512,768]{1...) while((s32[]{:T(128)}, bf16[3,256,768]{1,2,0:T(8,128)(2,1)}, ...), condition=%wide.region_14.15_spmd.clone, body=%wide.region_13.14_spmd.sunk.clone | while | flops 1020395520 | bytes 62632124 | solution.py:212
  325.2 3.7 fusion.152
  331.4 4.4 multiply_convert_fusion.4
  337.6 1.5 fusion.153
  342.3 3.7 fusion.152
  348.4 4.4 multiply_convert_fusion.4
  354.7 1.5 fusion.153
  359.3 3.7 fusion.152
  365.5 4.4 multiply_convert_fusion.4
  371.7 1.5 fusion.153
  377.1 2.5 fusion.60
  379.7 8.9 fusion.63
  388.7 6.8 fusion.66
  395.5 4.3 reduce-scatter.7.cloned.1.call-done
  399.8 3.2 convert_reduce_fusion.1
  403.0 5.2 convolution_bitcast_fusion
  408.2 2.7 copy-done.3
  410.9 24.4 %pad_maximum_fusion = f32[9216,768]{1,0:T(8,128)} fusion(f32[3072,768]{1,0:T(8,128)S(1)} %bitcast.199, f32[3072,768]{1,0:T(8,128)S(1)} %copy-done.3, f32[768,768]{1,0:T(8,128)} %fusion.60, f32[2304,768]{1,0:T(8,128)} %convolution_bitcast_fusion), kind=kLoop, calls=%fused_computation.32 | loop fusion | flops 21233664 | bytes 56623104 | tf_op jit(solution)/shard_map/concatenate | solution.py:246
  442.3 3.9 copy.64
  447.0 8.1 select_reduce_fusion
  456.4 379.1 %reduce-scatter.11.cloned.1.call-done = f32[576,768]{1,0:T(8,128)} async-done(((f32[9216,768]{1,0:T(8,128)}), f32[576,768]{1,0:T(8,128)}) %reduce-scatter.11.cloned.1.call-update) | async-done | bytes 1769488 | tf_op jit(solution)/shard_map/reduce_scatter | solution.py:264
  835.5 2.5 convert_element_type.131
  838.1 3.5 select_select_fusion.1
  841.6 119.7 %reduce-scatter.13.cloned.1.call-done = f32[48,13]{1,0:T(8,128)} async-done(((f32[768,13]{1,0:T(8,128)}), f32[48,13]{1,0:T(8,128)}) %reduce-scatter.13.cloned.1.call-update) | async-done | bytes 2512
  962.1 2.5 psum.22
  965.1 17.7 %all-reduce.2.cloned.1.call-done = bf16[576,768]{1,0:T(8,128)(2,1)} async-done(((bf16[576,768]{1,0:T(8,128)(2,1)}), bf16[576,768]{1,0:T(8,128)(2,1)}) %all-reduce.2.cloned.1.call-update) | async-done | bytes 884752 | tf_op jit(solution)/shard_map/psum | solution.py:268
  982.8 2.2 fusion.38
  986.4 70.4 %scatter_fusion = f32[3,256,768]{2,1,0:T(8,128)S(1)} fusion(f32[3,256,768]{2,1,0:T(8,128)S(1)} %get-tuple-element.245, s32[768]{0:T(1024)S(1)} %reshape.195, f32[768,768]{1,0:T(8,128)} %bitcast.200), kind=kCustom, calls=%fused_computation.1 | custom fusion | flops 589824 | bytes 7084032 | tf_op jit(solution)/shard_map/transpose(jvp(vmap()))/scatter-add | solution.py:48
  1056.8 42.5 %psum.23 = f32[]{:T(128)} all-reduce(f32[]{:T(128)S(6)} %add.188), channel_id=1, replica_groups=mesh['dp'=16,'seq'=2] {'dp'}, use_global_device_ids=true, to_apply=%region_33.34 | all-reduce | flops 1 | bytes 8 | tf_op jit(solution)/shard_map/psum | solution.py:271
  1100.7 6.1 fusion.72
  (233 shorter events, 53.7 us)
Async XLA Ops:
  7.2 2.7 copy-start.18
  7.2 46.8 %copy-start.12 = (bf16[3,256,768]{2,1,0:T(8,128)(2,1)S(1)}, bf16[3,256,768]{2,1,0:T(8,128)(2,1)}, u32[]{:S(2)}) copy-start(bf16[3,256,768]{2,1,0:T(8,128)(2,1)} %param.15) | copy-start | bytes 3538948
  7.2 174.2 %all-gather.5.cloned.1.call-start = ((), (), s32[]{:S(2)}) async-start(), calls=%async_computation.4 | async-start | bytes 15040512 | tf_op jit(solution)/shard_map/all_gather | solution.py:144
  9.8 44.4 %copy-start.39 = (s32[3,256]{1,0:T(4,128)S(1)}, s32[3,256]{1,0:T(4,128)}, u32[]{:S(2)}) copy-start(s32[3,256]{1,0:T(4,128)} %param.18) | copy-start | bytes 9220
  9.8 188.5 %all-gather.7.cloned.1.call-start = ((), (), s32[]{:S(2)}) async-start(), calls=%async_computation.5 | async-start | bytes 3538944 | tf_op jit(solution)/shard_map/all_gather | solution.py:166
  54.8 10.7 copy-start.29
  66.2 2.1 copy-start.23
  66.2 2.1 copy-start.35
  68.3 1.4 copy-start.4
  189.3 2.5 copy-start.1
  189.3 23.0 %all-gather.9.cloned.1.call-start = ((), (), s32[]{:S(2)}) async-start(), calls=%async_computation.6 | async-start | bytes 3538944 | tf_op jit(solution)/shard_map/all_gather | solution.py:165
  190.8 204.6 %reduce-scatter.9.cloned.1.call-start = ((), (), s32[]{:S(2)}) async-start(), calls=%async_computation.8 | async-start | bytes 3538944 | tf_op jit(solution)/shard_map/reduce_scatter | solution.py:227
  237.7 2.4 copy-start.5
  237.7 2.4 copy-start.43
  239.6 2.9 copy-start.16
  242.5 65.5 %copy-start.7 = (f32[768,768]{1,0:T(8,128)}, f32[768,768]{1,0:T(8,128)S(1)}, u32[]{:S(2)}) copy-start(f32[768,768]{1,0:T(8,128)S(1)} %get-tuple-element.251) | copy-start | bytes 7077892
  242.5 0.7 copy-start.40
  242.9 65.1 %copy-start.26 = (f32[768]{0:T(1024)}, f32[768]{0:T(1024)S(1)}, u32[]{:S(2)}) copy-start(f32[768]{0:T(1024)S(1)} %add_rsqrt_fusion.1) | copy-start | bytes 9220
  243.2 28.1 %copy-start.42 = (f32[768]{0:T(1024)S(1)}, f32[768]{0:T(1024)}, u32[]{:S(2)}) copy-start(f32[768]{0:T(1024)} %get-tuple-element.177) | copy-start | bytes 9220
  271.3 8.1 copy-start.44
  279.4 1.3 copy-start.2
  279.9 2.4 copy-start.20
  285.2 14.6 %copy-start.14 = (f32[768,768]{1,0:T(8,128)}, f32[768,768]{1,0:T(8,128)S(1)}, u32[]{:S(2)}) copy-start(f32[768,768]{1,0:T(8,128)S(1)} %get-tuple-element.225) | copy-start | bytes 7077892
  308.0 1.7 copy-start.9
  308.9 5.0 copy-start.10
  331.4 6.3 slice-start
  331.4 6.3 slice-start.1
  348.4 6.3 slice-start
  348.4 6.2 slice-start.1
  365.4 6.3 slice-start
  365.4 6.3 slice-start.1
  375.2 1.7 copy-start.11
  375.2 2.0 copy-start.17
  375.2 24.6 %reduce-scatter.7.cloned.1.call-start = ((), (), s32[]{:S(2)}) async-start(), calls=%async_computation.7 | async-start | bytes 3538944 | tf_op jit(solution)/shard_map/reduce_scatter | solution.py:224
  375.8 459.7 %reduce-scatter.11.cloned.1.call-start = ((), (), s32[]{:S(2)}) async-start(), calls=%async_computation.9 | async-start | bytes 30081024 | tf_op jit(solution)/shard_map/reduce_scatter | solution.py:264
  377.1 2.5 copy-start.15
  377.1 11.5 %slice-start.5 = ((s8[4718592]{0:T(1024)(128)(4,1)}), s8[4194304]{0:T(1024)(128)(4,1)S(1)}, s32[]{:S(2)}) async-start(s8[4718592]{0:T(1024)(128)(4,1)} %bitcast.215), calls=%async_computation.17 | async-start | bytes 8388608
  379.7 9.0 copy-start.8
  379.7 9.0 copy-start.27
  379.7 9.0 copy-start.41
  379.7 9.0 slice-start.6
  399.8 3.2 copy-start.6
  399.8 8.4 slice-start.2
  403.0 5.2 slice-start.3
  403.0 5.2 slice-start.4
  403.0 7.9 copy-start.3
  435.3 0.7 copy-start.24
  435.3 1.3 copy-start.21
  435.3 4.4 copy-start.22
  435.3 525.9 %reduce-scatter.13.cloned.1.call-start = ((), (), s32[]{:S(2)}) async-start(), calls=%async_computation.11 | async-start | bytes 417792
  446.9 8.1 copy-start.30
  446.9 8.1 copy-start.31
  446.9 8.1 copy-start.32
  446.9 8.1 copy-start.33
  447.0 8.1 copy-start.34
  455.0 383.0 %copy-start.28 = (s32[3,256,1]{1,0,2:T(4,128)S(1)}, s32[3,256,1]{1,0,2:T(4,128)}, u32[]{:S(2)}) copy-start(s32[3,256,1]{1,0,2:T(4,128)} %get-tuple-element.248) | copy-start | bytes 9220
  455.0 383.0 %copy-start.25 = (pred[3,256]{1,0:T(4,128)(4,1)S(1)}, pred[3,256]{1,0:T(4,128)(4,1)}, u32[]{:S(2)}) copy-start(pred[3,256]{1,0:T(4,128)(4,1)} %copy-done.23) | copy-start | bytes 2308
  455.0 383.0 %copy-start.36 = (pred[3,256]{1,0:T(4,128)(4,1)S(1)}, pred[3,256]{1,0:T(4,128)(4,1)}, u32[]{:S(2)}) copy-start(pred[3,256]{1,0:T(4,128)(4,1)} %copy-done.35) | copy-start | bytes 2308
  456.1 526.7 %all-reduce.2.cloned.1.call-start = ((), (), s32[]{:S(2)}) async-start(), calls=%async_computation.10 | async-start | bytes 1769472 | tf_op jit(solution)/shard_map/psum | solution.py:268
  986.3 113.7 %copy-start.19 = (f32[13,48]{1,0:T(8,128)S(1)}, f32[13,48]{1,0:T(8,128)}, u32[]{:S(2)}) copy-start(f32[13,48]{1,0:T(8,128)} %param.20) | copy-start | bytes 7492
  986.4 113.7 %copy-start.37 = (f32[13,48]{1,0:T(8,128)S(1)}, f32[13,48]{1,0:T(8,128)}, u32[]{:S(2)}) copy-start(f32[13,48]{1,0:T(8,128)} %param.23) | copy-start | bytes 7492
  986.4 113.7 %copy-start.38 = (f32[13,48]{1,0:T(8,128)S(1)}, f32[13,48]{1,0:T(8,128)}, u32[]{:S(2)}) copy-start(f32[13,48]{1,0:T(8,128)} %param.24) | copy-start | bytes 7492
  986.4 114.3 %copy-start.13 = (bf16[576,768]{1,0:T(8,128)(2,1)S(1)}, bf16[576,768]{1,0:T(8,128)(2,1)}, u32[]{:S(2)}) copy-start(bf16[576,768]{1,0:T(8,128)(2,1)} %all-reduce.2.cloned.1.call-done) | copy-start | bytes 2654212
  1056.8 50.0 %copy-start = (f32[3,256,768]{2,1,0:T(8,128)}, f32[3,256,768]{2,1,0:T(8,128)S(1)}, u32[]{:S(2)}) copy-start(f32[3,256,768]{2,1,0:T(8,128)S(1)} %scatter_fusion) | copy-start | bytes 7077892
Sparse Core Ops, SparseCore 0:
  11.4 169.9 all-gather.4
  189.4 8.8 all-gather.6
  200.4 11.8 all-gather.8
  375.3 11.1 reduce-scatter.8
  388.6 11.0 reduce-scatter.6
  435.5 400.0 reduce-scatter.10
  840.7 120.4 reduce-scatter.12
  964.3 18.4 all-reduce.1
where the time goes:
time: 1120 us
  waiting for transfers between devices  651 us (58%)
  matrix products  148 us (13%)
  other arithmetic  136 us (12%)
  blocking collectives  88.2 us (8%)
  local copies, waits for them, and re-layouts  72.2 us (6%)
  between operations  18.1 us (2%)
    reduce_scatter x1, waiting for transfers between devices, shards(): lax.psum_scatter(flat_grad, 'dp', scatter_dimension=0, tiled=True)  379 us
    unnamed x9, waiting for transfers between devices  120 us
    all_gather x1, waiting for transfers between devices, shards(): lax.all_gather(low_weights, 'dp', axis=0, tiled=True)  112 us
    scatter-add x1, other arithmetic, corrupt(): seq_rows[where_from]  70.4 us
    all_gather x1, blocking collectives, shards(): lax.all_gather(low_vectors, 'dp', axis=1, tiled=True)  43.3 us
    psum x1, blocking collectives, shards(): lax.psum(jnp.sum(shard_w * shard_w) + jnp.sum(shard_v * shard_v), 'dp')  42.5 us
    dot_general x1, matrix products, shards(): jnp.einsum('rd,fd->rf', hidden_low, w_in, preferred_element_type=jnp.floa...  28 us
    concatenate x1, other arithmetic, shards(): jnp.concatenate([grad_qkv_w, grad_out_w, grad_in_w, grad_down_w], axis=0)  24.4 us
  transfers between devices with their start and end apart: 8, of which 7 were waited for; matrix products, arithmetic and copies ran while one was open for 6% of the time, Pallas kernels for 0%

commit v1 on v0

v1 whole, which is shorter than its diff:
```python
import functools

import jax
import jax.numpy as jnp
from jax import lax
from jax.experimental import pallas as pl
from jax.experimental.pallas import tpu as pltpu
from jax.sharding import PartitionSpec as P

D = 768
HEADS = 12
HEAD_DIM = 64
FF = 3072
STEP = 10
CHUNK = 96
OWN = D // 2
UNITS = FF // 2

ln_eps = 1e-12
beta_one = 0.9
beta_two = 0.999
adam_eps = 1e-08
learn_rate = 0.05
vector_rate = 0.3
decay_rate = 0.01

bf16 = jnp.bfloat16
f32 = jnp.float32
SWAP = [(0, 1), (1, 0)]


def params(limit=48):
    return pltpu.CompilerParams(vmem_limit_bytes=limit * 2**20)


def dot(left, right, over):
    return lax.dot_general(left, right, (over, ((), ())), preferred_element_type=f32)


NT = ((1,), (1,))
NN = ((1,), (0,))
TN = ((0,), (0,))


def swap(value):
    return lax.ppermute(value, "seq", SWAP)


def other_half(array, axis=0):
    half = array.shape[axis] // 2
    return lax.slice_in_dim(array, half, 2 * half, axis=axis)


def pack(rows, index):
    core = lax.axis_index("seq")
    chunks = rows.shape[0] // (2 * CHUNK)
    plain = lax.dynamic_index_in_dim(rows.reshape(chunks, 2, CHUNK, D), core, 1, keepdims=False)
    columns = lax.dynamic_slice_in_dim(rows, core * OWN, OWN, axis=1).reshape(chunks, 2, CHUNK, OWN)
    wide = jnp.concatenate([columns[:, 0], columns[:, 1]], axis=-1)
    where = index * chunks + jnp.arange(chunks)
    is_out = ((where >= 12) & (where < 16))[:, None, None]
    return jnp.where(is_out, wide, plain).reshape(chunks * CHUNK, D)


def unpack(mine, theirs, index):
    core = lax.axis_index("seq")
    chunks = mine.shape[0] // CHUNK
    first = jnp.where(core == 0, mine, theirs).reshape(chunks, CHUNK, D)
    second = jnp.where(core == 0, theirs, mine).reshape(chunks, CHUNK, D)
    plain = jnp.stack([first, second], axis=1)
    upper = jnp.concatenate([first[..., :OWN], second[..., :OWN]], axis=-1)
    lower = jnp.concatenate([first[..., OWN:], second[..., OWN:]], axis=-1)
    wide = jnp.stack([upper, lower], axis=1)
    where = index * chunks + jnp.arange(chunks)
    is_out = ((where >= 12) & (where < 16))[:, None, None, None]
    return jnp.where(is_out, wide, plain).reshape(chunks * 2 * CHUNK, D)


SIDE_X = [(i, i ^ 1) for i in range(16)]
SIDE_Y = [(i, i ^ 2) for i in range(16)]


def up(first, last):
    return [(i, i + 4) for i in range(16) if first <= i // 4 <= last]


def down(first, last):
    return [(i, i - 4) for i in range(16) if first <= i // 4 <= last]


def send(value, pairs):
    return lax.ppermute(value, "dp", pairs)


def pick(plane, *options):
    result = options[-1]
    for i in range(len(options) - 2, -1, -1):
        result = jnp.where(plane == i, options[i], result)
    return result


def in_plane(block):
    half = block.shape[0] // 2
    over_x = send(block, SIDE_X)
    over_y = send(block, SIDE_Y)
    over_xy = jnp.concatenate([send(over_x[:half], SIDE_Y), send(over_y[half:], SIDE_X)], axis=0)
    return (block, over_x, over_y, over_xy)


def place_kernel(piece, me_ref, *refs):
    out_ref, sems = refs[-2], refs[-1]
    slots = [refs[4 * i : 4 * i + 4] for i in range((len(refs) - 2) // 4)]
    me = me_ref[0]
    plane = me // 4
    spot = me % 4
    for z in range(4):
        order = [z] + [i for i in range(4) if i != z]
        slot = order.index(piece)
        if slot >= len(slots):
            continue

        @pl.when(plane == z)
        def _():
            copies = []
            for side in range(4):
                place = side + spot - 2 * (side & spot)
                copies.append(
                    pltpu.make_async_copy(slots[slot][side], out_ref.at[place], sems.at[side])
                )
            for copy in copies:
                copy.start()
            for copy in copies:
                copy.wait()


def place(piece, me, slots):
    flat = [block for slot in slots for block in slot]
    rows = flat[0].shape[0]
    return pl.pallas_call(
        functools.partial(place_kernel, piece),
        in_specs=[pl.BlockSpec(memory_space=pltpu.SMEM)]
        + [pl.BlockSpec(memory_space=pl.ANY)] * len(flat),
        out_specs=pl.BlockSpec(memory_space=pl.ANY),
        out_shape=jax.ShapeDtypeStruct((4, rows, D), bf16),
        scratch_shapes=[pltpu.SemaphoreType.DMA((4,))],
        cost_estimate=pl.CostEstimate(flops=0, bytes_accessed=8 * rows * D * 2, transcendentals=0),
        name="place",
    )(me, *flat).reshape(4 * rows, D)


def gather_pieces(block):
    index = lax.axis_index("dp")
    plane = index // 4
    me = index.reshape(1)
    rise1 = send(block, up(0, 2))
    fall1 = send(block, down(1, 3))
    slot0 = in_plane(block)
    rise2 = send(rise1, up(1, 2))
    fall2 = send(fall1, down(1, 2))
    rise3 = send(rise2, up(2, 2))
    fall3 = send(fall2, down(1, 1))
    slot1 = in_plane(pick(plane, fall1, rise1, rise2, rise3))
    slot2 = in_plane(pick(plane, fall2, fall1, rise1, rise2))
    slot3 = in_plane(pick(plane, fall3, fall2, fall1, rise1))
    return [
        place(0, me, (slot0, slot1)),
        place(1, me, (slot0, slot1, slot2)),
        place(2, me, (slot0, slot1, slot2, slot3)),
        place(3, me, (slot0, slot1, slot2, slot3)),
    ]


def plus(*values):
    total = values[0].astype(f32)
    for value in values[1:]:
        total = total + value.astype(f32)
    return total.astype(bf16)


def reduce_in_plane(piece, spot):
    blocks = piece.reshape(4, -1, D)
    own, side_x, side_y, side_xy = (
        lax.dynamic_index_in_dim(blocks, spot ^ i, 0, keepdims=False) for i in range(4)
    )
    half = own.shape[0] // 2
    from_y = send(side_xy[:half], SIDE_Y)
    from_x = send(side_xy[half:], SIDE_X)
    side_x = jnp.concatenate([plus(side_x[:half], from_y), side_x[half:]], axis=0)
    side_y = jnp.concatenate([side_y[:half], plus(side_y[half:], from_x)], axis=0)
    return plus(own, send(side_x, SIDE_X), send(side_y, SIDE_Y))


def reduce_pieces(pieces, index):
    plane, spot = index // 4, index % 4
    three, two, one, zero = (reduce_in_plane(piece, spot) for piece in pieces)
    three = plus(three, send(three, up(0, 0)))
    three = plus(three, send(three, up(1, 1)))
    three = plus(three, send(three, up(2, 2)))
    two = plus(two, send(two, up(0, 0) + down(3, 3)))
    two = plus(two, send(two, up(1, 1)))
    one = plus(one, send(one, down(3, 3) + up(0, 0)))
    one = plus(one, send(one, down(2, 2)))
    zero = plus(zero, send(zero, down(3, 3)))
    zero = plus(zero, send(zero, down(2, 2)))
    zero = plus(zero, send(zero, down(1, 1)))
    return pick(plane, zero, one, two, three)


def sum_ranks(value, ranks):
    if ranks & (ranks - 1):
        return lax.psum(value, ("dp", "seq"))
    value = value + swap(value)
    step = 1
    while step < ranks:
        value = value + lax.ppermute(value, "dp", [(i, i ^ step) for i in range(ranks)])
        step *= 2
    return value


def gather_vectors(low_vectors, ranks):
    if ranks & (ranks - 1):
        return lax.all_gather(low_vectors, "dp", axis=1, tiled=True).astype(f32)
    count, width = low_vectors.shape
    index = lax.axis_index("dp")
    spread = jnp.zeros((ranks, count, width), bf16)
    spread = lax.dynamic_update_slice(spread, low_vectors[None], (index, 0, 0))
    spread = spread.transpose(1, 0, 2).reshape(count, ranks * width)
    step = 1
    while step < ranks:
        spread = spread + lax.ppermute(spread, "dp", [(i, i ^ step) for i in range(ranks)])
        step *= 2
    return spread.astype(f32)


def selection(span, kind, source, half_len):
    chosen = span == 1
    masked = chosen & (kind < 8)
    swapped = chosen & (kind == 8)
    here = lax.broadcasted_iota(jnp.int32, (1, half_len), 1)
    origin = jnp.where(masked, -1, jnp.where(swapped, source, here))
    rows = lax.broadcasted_iota(jnp.int32, (half_len, half_len), 0)
    one_hot = (rows == origin).astype(f32).astype(bf16)
    first = lax.broadcasted_iota(jnp.int32, (16, half_len), 0) == 0
    mask_rows = jnp.where(first & masked, 1.0, 0.0).astype(bf16)
    return one_hot, mask_rows


def corrupt_kernel(span_ref, kind_ref, from_ref, hidden_ref, mask_ref, out_ref):
    seqs, half_len = span_ref.shape
    for s in range(seqs):
        rows = slice(s, s + 1)
        one_hot, mask_rows = selection(
            span_ref[rows, :], kind_ref[rows, :], from_ref[rows, :], half_len
        )
        picked = dot(one_hot, hidden_ref[s], TN) + dot(mask_rows, mask_ref[...], TN)
        out_ref[s] = picked.astype(bf16)


def corrupt(span, kind, source, hidden, mask_row):
    mask = jnp.broadcast_to(mask_row.astype(bf16)[None], (16, D))
    return pl.pallas_call(
        corrupt_kernel,
        out_shape=jax.ShapeDtypeStruct(hidden.shape, bf16),
        compiler_params=params(),
        name="corrupt",
    )(span, kind, source, hidden, mask)


def corrupt_back_kernel(span_ref, kind_ref, from_ref, grad_ref, partial_ref, out_ref, mask_ref):
    seqs, half_len = span_ref.shape
    mask_sum = jnp.zeros((16, D), f32)
    for s in range(seqs):
        rows = slice(s, s + 1)
        one_hot, mask_rows = selection(
            span_ref[rows, :], kind_ref[rows, :], from_ref[rows, :], half_len
        )
        grad = grad_ref[s] + partial_ref[s].astype(f32)
        high = grad.astype(bf16)
        low = (grad - high.astype(f32)).astype(bf16)
        out_ref[s] = dot(one_hot, high, NN) + dot(one_hot, low, NN)
        mask_sum = mask_sum + dot(mask_rows, high, NN) + dot(mask_rows, low, NN)
    mask_ref[...] = mask_sum


def corrupt_back(span, kind, source, grad, partial):
    return pl.pallas_call(
        corrupt_back_kernel,
        out_shape=[
            jax.ShapeDtypeStruct(grad.shape, f32),
            jax.ShapeDtypeStruct((16, D), f32),
        ],
        compiler_params=params(),
        name="corrupt_back",
    )(span, kind, source, grad, partial)


def attend_kernel(u_ref, w_ref, bias_ref, qkv_ref, low_ref, wide_ref, lse_ref):
    half_len = u_ref.shape[2]
    rows = u_ref[:, 0].reshape(2 * half_len, D)
    projected = (dot(rows, w_ref[...], NT) + bias_ref[...]).astype(bf16)
    qkv_ref[:, 0] = projected.reshape(2, half_len, 3 * OWN)
    wide, totals = [], []
    for h in range(OWN // HEAD_DIM):
        columns = slice(h * HEAD_DIM, (h + 1) * HEAD_DIM)
        query = projected[:, :OWN][:, columns] * bf16(HEAD_DIM**-0.5)
        key = projected[:, OWN : 2 * OWN][:, columns]
        value = projected[:, 2 * OWN :][:, columns]
        scores = dot(query, key, NT)
        top = jnp.max(scores, axis=-1, keepdims=True)
        exponents = jnp.exp(scores - top)
        total = jnp.sum(exponents, axis=-1, keepdims=True)
        probabilities = (exponents / total).astype(bf16)
        wide.append(dot(probabilities, value, NN))
        totals.append(top + jnp.log(total))
    attended = jnp.concatenate(wide, axis=-1)
    wide_ref[:, 0] = attended.reshape(2, half_len, OWN)
    low_ref[:, 0] = attended.astype(bf16).reshape(2, half_len, OWN)
    fill = jnp.zeros((2 * half_len, 128 - len(totals)), f32)
    lse_ref[0] = jnp.concatenate(totals + [fill], axis=-1).T[:8]


def attend(u_all, w_own, bias):
    _, seqs, half_len, _ = u_all.shape
    block = lambda width: pl.BlockSpec((2, 1, half_len, width), lambda s: (0, s, 0, 0))
    flops = seqs * (2 * 512 * D * 3 * OWN + 4 * 6 * 512 * 512 * 256)
    return pl.pallas_call(
        attend_kernel,
        grid=(seqs,),
        in_specs=[
            block(D),
            pl.BlockSpec((3 * OWN, D), lambda s: (0, 0)),
            pl.BlockSpec((1, 3 * OWN), lambda s: (0, 0)),
        ],
        out_specs=[
            block(3 * OWN),
            block(OWN),
            block(OWN),
            pl.BlockSpec((1, 8, 2 * half_len), lambda s: (s, 0, 0)),
        ],
        out_shape=[
            jax.ShapeDtypeStruct((2, seqs, half_len, 3 * OWN), bf16),
            jax.ShapeDtypeStruct((2, seqs, half_len, OWN), bf16),
            jax.ShapeDtypeStruct((2, seqs, half_len, OWN), f32),
            jax.ShapeDtypeStruct((seqs, 8, 2 * half_len), f32),
        ],
        cost_estimate=pl.CostEstimate(
            flops=flops, bytes_accessed=12 * 2**20, transcendentals=seqs * 6 * 512 * 512
        ),
        compiler_params=params(),
        name="attend",
    )(u_all, w_own, bias)


def attend_back_kernel(qkv_ref, grad_ref, wo_ref, wide_ref, lse_ref, out_ref, sums_ref):
    half_len = qkv_ref.shape[2]
    length = 2 * half_len
    projected = qkv_ref[:, 0].reshape(length, 3 * OWN)
    grad = dot(grad_ref[:, 0].reshape(length, D), wo_ref[...], NN).astype(bf16)
    product = grad.astype(f32) * wide_ref[:, 0].reshape(length, OWN)
    heads = OWN // HEAD_DIM
    deltas = [
        jnp.sum(product[:, h * HEAD_DIM : (h + 1) * HEAD_DIM], axis=-1, keepdims=True)
        for h in range(heads)
    ]
    fill = jnp.zeros((length, 128 - heads), f32)
    delta_rows = jnp.concatenate(deltas + [fill], axis=-1).T
    parts = [[], [], []]
    for h in range(heads):
        columns = slice(h * HEAD_DIM, (h + 1) * HEAD_DIM)
        query = projected[:, :OWN][:, columns] * bf16(HEAD_DIM**-0.5)
        key = projected[:, OWN : 2 * OWN][:, columns]
        value = projected[:, 2 * OWN :][:, columns]
        grad_head = grad[:, columns]
        weights = jnp.exp(dot(key, query, NT) - lse_ref[0, h : h + 1, :])
        grad_weights = dot(value, grad_head, NT)
        grad_scores = (weights * (grad_weights - delta_rows[h : h + 1, :])).astype(bf16)
        parts[0].append(dot(grad_scores, key, TN) * HEAD_DIM**-0.5)
        parts[1].append(dot(grad_scores, query, NN))
        parts[2].append(dot(weights.astype(bf16), grad_head, NN))
    result = jnp.concatenate(parts[0] + parts[1] + parts[2], axis=-1).astype(bf16)
    out_ref[:, 0] = result.reshape(2, half_len, 3 * OWN)
    sums = jnp.sum(result.astype(f32), axis=0, keepdims=True)

    @pl.when(pl.program_id(0) == 0)
    def _():
        sums_ref[...] = jnp.zeros_like(sums_ref)

    sums_ref[...] += sums


def attend_back(qkv, grad_all, wo_own, wide, lse):
    _, seqs, half_len, _ = qkv.shape
    block = lambda width: pl.BlockSpec((2, 1, half_len, width), lambda s: (0, s, 0, 0))
    flops = seqs * (2 * 512 * D * OWN + 10 * 6 * 512 * 512 * 256)
    return pl.pallas_call(
        attend_back_kernel,
        grid=(seqs,),
        in_specs=[
            block(3 * OWN),
            block(D),
            pl.BlockSpec((D, OWN), lambda s: (0, 0)),
            block(OWN),
            pl.BlockSpec((1, 8, 2 * half_len), lambda s: (s, 0, 0)),
        ],
        out_specs=[block(3 * OWN), pl.BlockSpec((1, 3 * OWN), lambda s: (0, 0))],
        out_shape=[
            jax.ShapeDtypeStruct((2, seqs, half_len, 3 * OWN), bf16),
            jax.ShapeDtypeStruct((1, 3 * OWN), f32),
        ],
        cost_estimate=pl.CostEstimate(
            flops=flops, bytes_accessed=12 * 2**20, transcendentals=seqs * 6 * 512 * 512
        ),
        compiler_params=params(),
        name="attend_back",
    )(qkv, grad_all, wo_own, wide, lse)


def hidden_kernel(h_ref, w_ref, bias_ref, gelu_ref, slope_ref):
    points = dot(h_ref[...], w_ref[...], NT) + bias_ref[...]
    below = 0.5 * (1.0 + lax.erf(points * 2**-0.5))
    density = jnp.exp(-0.5 * points * points) * 0.3989422804014327
    gelu_ref[...] = (points * below).astype(bf16)
    slope_ref[...] = (below + points * density).astype(bf16)


def hidden_units(h_rows, w_in, bias):
    rows = h_rows.shape[0]
    units = w_in.shape[0]
    width = 256
    block = pl.BlockSpec((rows, width), lambda i: (0, i))
    return pl.pallas_call(
        hidden_kernel,
        grid=(units // width,),
        in_specs=[
            pl.BlockSpec((rows, D), lambda i: (0, 0)),
            pl.BlockSpec((width, D), lambda i: (i, 0)),
            pl.BlockSpec((1, width), lambda i: (0, i)),
        ],
        out_specs=[block, block],
        out_shape=[jax.ShapeDtypeStruct((rows, units), bf16)] * 2,
        cost_estimate=pl.CostEstimate(
            flops=2 * rows * units * D,
            bytes_accessed=4 * rows * units + 2 * rows * D,
            transcendentals=2 * rows * units,
        ),
        compiler_params=params(),
        name="hidden_units",
    )(h_rows, w_in, bias)


def norm(values):
    center = values - jnp.mean(values, axis=-1, keepdims=True)
    inv_std = lax.rsqrt(jnp.mean(center * center, axis=-1, keepdims=True) + ln_eps)
    return center * inv_std, inv_std


def norm_backward(upstream, normed, inv_std, gain):
    scaled = upstream * gain
    return inv_std * (
        scaled
        - jnp.mean(scaled, axis=-1, keepdims=True)
        - normed * jnp.mean(scaled * normed, axis=-1, keepdims=True)
    )


def adam_step(master, first_old, second, gradient, decay_on, step_rate):
    first_new = beta_one * first_old + (1.0 - beta_one) * gradient
    second_new = beta_two * second + (1.0 - beta_two) * gradient * gradient
    fix_one = 1.0 - beta_one**STEP
    fix_two = 1.0 - beta_two**STEP
    update = first_new / fix_one / (jnp.sqrt(second_new / fix_two) + adam_eps)
    return (master - step_rate * (update + decay_on * master), first_new, second_new)


def own_columns(value):
    return lax.dynamic_slice_in_dim(value, lax.axis_index("seq") * OWN, OWN, axis=value.ndim - 1)


def shards(
    ranks,
    hidden,
    span_mask,
    replace_kind,
    replace_from,
    weights,
    vectors,
    weight_first,
    weight_second,
    vector_first,
    vector_second,
    cotangent,
):
    seqs, half_len, _ = hidden.shape
    rows = seqs * half_len
    index = lax.axis_index("dp")
    core = lax.axis_index("seq")

    low_weights = weights.astype(bf16)
    vals = gather_vectors(vectors.astype(bf16), ranks)
    if ranks == 16:
        pieces = gather_pieces(pack(low_weights, index))
    else:
        whole = pack(lax.all_gather(low_weights, "dp", axis=0, tiled=True), 0)
        pieces = [whole[i * 12 * CHUNK : (i + 1) * 12 * CHUNK] for i in range(4)]
    piece0, piece1, piece2, piece3 = pieces

    u_own = corrupt(span_mask, replace_kind, replace_from, hidden, vals[8])
    u_all = jnp.stack([u_own, swap(u_own)])

    halves = piece0.reshape(3, 2, 2, CHUNK, D)
    mine = lax.dynamic_index_in_dim(halves, core, 1, keepdims=False)
    theirs = swap(lax.dynamic_index_in_dim(halves, 1 - core, 1, keepdims=False))
    w_qkv = jnp.where(
        core == 0, jnp.stack([mine, theirs], axis=2), jnp.stack([theirs, mine], axis=2)
    ).reshape(3 * OWN, D)
    bias = jnp.concatenate(
        [own_columns(vals[0:1]), jnp.zeros((1, OWN), f32), own_columns(vals[1:2])], axis=-1
    )
    qkv, attended, attended_wide, lse = attend(u_all, w_qkv, bias)

    out_pack = piece1[: 4 * CHUNK].reshape(4, CHUNK, 2, OWN)
    wo_own = out_pack.transpose(0, 2, 1, 3).reshape(D, OWN)
    wo_other = swap(wo_own)
    from_other = swap(attended[1]).reshape(rows, OWN)
    branch = (
        dot(attended[0].reshape(rows, OWN), wo_own, NT) + dot(from_other, wo_other, NT) + vals[2]
    )
    normed_one, inv_one = norm(u_own.reshape(rows, D).astype(f32) + branch)
    hidden_one = normed_one * vals[3] + vals[4]
    h_low = hidden_one.astype(bf16)
    h_all = jnp.concatenate([h_low, swap(h_low)], axis=0)

    bias_in = lax.dynamic_index_in_dim(
        vals[9:].reshape(FF // (2 * CHUNK), 2, CHUNK), core, 1, keepdims=False
    ).reshape(1, UNITS)
    half_units = UNITS // 2
    w_in = jnp.concatenate([piece1[4 * CHUNK :], piece2[: 8 * CHUNK]], axis=0)
    gelu_a, slope_a = hidden_units(h_all, piece1[4 * CHUNK :], bias_in[:, :half_units])
    gelu_b, slope_b = hidden_units(h_all, piece2[: 8 * CHUNK], bias_in[:, half_units:])
    gelu = jnp.concatenate([gelu_a, gelu_b], axis=1)
    slope = jnp.concatenate([slope_a, slope_b], axis=1)
    w_down = jnp.concatenate([piece2[8 * CHUNK :], piece3], axis=0)
    feed_other = swap(dot(gelu[rows:], w_down, NN).astype(bf16))
    feed = dot(gelu[:rows], w_down, NN) + feed_other.astype(f32) + vals[5]
    normed_two, inv_two = norm(hidden_one + feed)
    layer_out = normed_two * vals[6] + vals[7]

    grad_out = cotangent.astype(f32).reshape(rows, D)
    grad_two = norm_backward(grad_out, normed_two, inv_two, vals[6])
    grad_feed = grad_two.astype(bf16)
    grad_feed_all = jnp.concatenate([grad_feed, swap(grad_feed)], axis=0)
    grad_down = dot(gelu, grad_feed_all, TN).astype(bf16)
    grad_pre = (dot(grad_feed_all, w_down, NT) * slope.astype(f32)).astype(bf16)
    grad_in = dot(grad_pre, h_all, TN).astype(bf16)
    sent_hidden = swap(dot(grad_pre[rows:], w_in, NN).astype(bf16))
    grad_hidden = grad_two + dot(grad_pre[:rows], w_in, NN) + sent_hidden.astype(f32)
    grad_one = norm_backward(grad_hidden, normed_one, inv_one, vals[3])
    grad_branch = grad_one.astype(bf16)
    grad_branch_all = jnp.concatenate([grad_branch, swap(grad_branch)], axis=0)
    grad_wo = dot(grad_branch_all, attended.reshape(2 * rows, OWN), TN).astype(bf16)
    grad_out_pack = (
        grad_wo.reshape(4, 2, CHUNK, OWN).transpose(0, 2, 1, 3).reshape(4 * CHUNK, D)
    )
    grad_qkv, qkv_sums = attend_back(
        qkv, grad_branch_all.reshape(2, seqs, half_len, D), wo_own, attended_wide, lse
    )
    grad_rows = grad_qkv.reshape(2 * rows, 3 * OWN)
    grad_proj = dot(grad_rows, u_all.reshape(2 * rows, D), TN).astype(bf16)
    sent_inputs = swap(dot(grad_rows[rows:], w_qkv, NN).astype(bf16))
    grad_inputs = grad_one + dot(grad_rows[:rows], w_qkv, NN)
    input_grad, grad_mask = corrupt_back(
        span_mask,
        replace_kind,
        replace_from,
        grad_inputs.reshape(seqs, half_len, D),
        sent_inputs.reshape(seqs, half_len, D),
    )

    halves = grad_proj.reshape(3, 2, 2, CHUNK, D)
    keep = lax.dynamic_index_in_dim(halves, core, 2, keepdims=False)
    give = swap(lax.dynamic_index_in_dim(halves, 1 - core, 2, keepdims=False))
    grad_zero = jnp.where(
        core == 0, jnp.stack([keep, give], axis=1), jnp.stack([give, keep], axis=1)
    ).reshape(12 * CHUNK, D)
    grad_pieces = [
        grad_down[4 * CHUNK :],
        jnp.concatenate([grad_in[8 * CHUNK :], grad_down[: 4 * CHUNK]], axis=0),
        jnp.concatenate([grad_out_pack, grad_in[: 8 * CHUNK]], axis=0),
        grad_zero,
    ]
    if ranks == 16:
        shard_half = reduce_pieces(grad_pieces, index)
        shard_w = unpack(shard_half, swap(shard_half), index).astype(f32)
    else:
        core_rows = jnp.concatenate(grad_pieces[::-1], axis=0)
        whole = unpack(core_rows, swap(core_rows), 0).astype(f32)
        shard_w = lax.psum_scatter(whole, "dp", scatter_dimension=0, tiled=True)
        shard_half = lax.dynamic_slice_in_dim(shard_w, core * OWN, OWN, axis=1)

    def at_own(value, width, step):
        spread = jnp.zeros((1, width), f32)
        return lax.dynamic_update_slice(spread, value, (0, core * step))

    bias_rows = jnp.zeros((FF // (2 * CHUNK), 2, CHUNK), f32)
    bias_rows = lax.dynamic_update_slice(
        bias_rows,
        jnp.sum(grad_pre.astype(f32), axis=0).reshape(FF // (2 * CHUNK), 1, CHUNK),
        (0, core, 0),
    ).reshape(FF // D, D)
    vector_rows = jnp.concatenate(
        [
            at_own(qkv_sums[:, :OWN], D, OWN),
            at_own(qkv_sums[:, 2 * OWN :], D, OWN),
            jnp.stack(
                [
                    jnp.sum(grad_branch.astype(f32), axis=0),
                    jnp.sum(grad_hidden * normed_one, axis=0),
                    jnp.sum(grad_hidden, axis=0),
                    jnp.sum(grad_feed.astype(f32), axis=0),
                    jnp.sum(grad_out * normed_two, axis=0),
                    jnp.sum(grad_out, axis=0),
                ]
            ),
            grad_mask[:1],
            bias_rows,
        ],
        axis=0,
    )
    vector_grad = sum_ranks(vector_rows, ranks)
    width = vectors.shape[1]
    shard_v = lax.dynamic_slice_in_dim(vector_grad, index * width, width, axis=1)

    half32 = shard_half.astype(f32)
    squares = sum_ranks(jnp.sum(half32 * half32).reshape(1, 1), ranks)[0, 0]
    grad_norm = jnp.sqrt(squares + jnp.sum(vector_grad * vector_grad))
    clip = 1.0 / jnp.maximum(grad_norm, 1.0)
    weights_new, weight_first_new, weight_second_new = adam_step(
        weights, weight_first, weight_second, shard_w * clip, decay_rate, learn_rate
    )
    vectors_new, vector_first_new, vector_second_new = adam_step(
        vectors, vector_first, vector_second, shard_v * clip, 0.0, vector_rate
    )
    return (
        layer_out.reshape(seqs, half_len, D),
        input_grad,
        grad_norm,
        weights_new,
        weight_first_new,
        weight_second_new,
        vectors_new,
        vector_first_new,
        vector_second_new,
        weights_new.astype(bf16),
        vectors_new.astype(bf16),
    )


def solution(mesh):
    token = P("dp", "seq", None)
    by_row = P("dp", None)
    by_column = P(None, "dp")
    position = P("dp", "seq")
    in_specs = (
        (token,) + (position,) * 3 + (by_row, by_column, by_row, by_row, by_column, by_column, token)
    )
    out_specs = (token, token, P()) + (by_row,) * 3 + (by_column,) * 3 + (by_row, by_column)
    return jax.shard_map(
        functools.partial(shards, mesh.shape["dp"]),
        mesh=mesh,
        in_specs=in_specs,
        out_specs=out_specs,
        check_vma=False,
    )
```

time: 1120 us -> 653 us (0.58)
  waiting for transfers between devices: 651 us -> 126 us
  Pallas kernels: 0 us -> 273 us
  matrix products: 148 us -> 49 us
  other arithmetic: 136 us -> 44.1 us
  starting transfers between devices: 0.72 us -> 90.8 us
  blocking collectives: 88.2 us -> 0 us
  local copies, waits for them, and re-layouts: 72.2 us -> 55 us
    reduce_scatter x3 -> x0, waiting for transfers between devices: 383 us -> none  [the longest x1 379 us: shards(): lax.psum_scatter(flat_grad, 'dp', scatter_dimension=0, tiled=True)]
    pallas_call x0 -> x10, Pallas kernels: none -> 273 us  [the longest x4 219 us: place(): pl.pallas_call(functools.partial(place_kernel, piece), in_specs=[pl.Block...]
    all_gather x3 -> x0, waiting for transfers between devices: 129 us -> none  [the longest x1 112 us: shards(): lax.all_gather(low_weights, 'dp', axis=0, tiled=True)]
    ppermute x0 -> x74, waiting for transfers between devices: none -> 126 us  [the longest x48 94.9 us: send(): return lax.ppermute(value, 'dp', pairs)]
    unnamed x9 -> x0, waiting for transfers between devices: 120 us -> none
    dot_general x33 -> x13, matrix products: 148 us -> 49 us  [dot(): lax.dot_general(left, right, (over, ((), ())), preferred_element_type=f32)]
    ppermute x0 -> x74, starting transfers between devices: none -> 90.8 us  [the longest x48 65.5 us: send(): return lax.ppermute(value, 'dp', pairs)]
    scatter-add x1 -> x0, other arithmetic: 70.4 us -> none  [corrupt(): seq_rows[where_from]]
  transfers between devices with their start and end apart: 8 -> 74, of which waited for: 7 -> 39; matrix products, arithmetic and copies ran while one was open for 6% -> 13% of each run, Pallas kernels for 0% -> 40%
where the time goes in v1:
time: 653 us; the launch traced here: 647 us
  Pallas kernels  273 us (42%)
  waiting for transfers between devices  126 us (19%)
  starting transfers between devices  90.8 us (14%)
  local copies, waits for them, and re-layouts  55 us (8%)
  matrix products  49 us (8%)
  other arithmetic  44.1 us (7%)
  between operations  8.64 us (1%)
    pallas_call x4, Pallas kernels, place(): pl.pallas_call(functools.partial(place_kernel, piece), in_specs=[pl.Block...  219 us
    ppermute x48, waiting for transfers between devices, send(): return lax.ppermute(value, 'dp', pairs)  94.9 us
    ppermute x48, starting transfers between devices, send(): return lax.ppermute(value, 'dp', pairs)  65.5 us
    dot_general x13, matrix products, dot(): lax.dot_general(left, right, (over, ((), ())), preferred_element_type=f32)  49 us
    pallas_call x1, Pallas kernels, attend_back(): pl.pallas_call(attend_back_kernel, grid=(seqs,), in_specs=[block(3 * OWN)...  23.9 us
    ppermute x8, starting transfers between devices, sum_ranks(): lax.ppermute(value, 'dp', [(i, i ^ step) for i in range(ranks)])  18.4 us
    unnamed x164, local copies, waits for them, and re-layouts  16.1 us
    pallas_call x1, Pallas kernels, attend(): pl.pallas_call(attend_kernel, grid=(seqs,), in_specs=[block(D), pl.BlockS...  15 us
  transfers between devices with their start and end apart: 74, of which 39 were waited for; matrix products, arithmetic and copies ran while one was open for 13% of the time, Pallas kernels for 40%

profile of v1, /device:TPU:0, one launch (start us, length us, event | category | flops | bytes accessed | tf_op | source)
XLA Modules:
  0.0 646.7 jit_solution(16011092974318199166)
XLA Ops:
  3.3 5.0 collective-permute-start.10
  9.5 8.1 %collective-permute-done.10 = bf16[288,768]{1,0:T(8,128)(2,1)S(1)} collective-permute-done((bf16[288,768]{1,0:T(8,128)(2,1)S(1)}, bf16[288,768]{1,0:T(8,128)(2,1)S(1)}, u32[]{:S(2)}, u32[]{:S(2)}) %collective-permute-start.10) | collective-permute-done | bytes 442400 | tf_op jit(solution)/shard_map/ppermute | solution.py:92
  18.3 3.5 collective-permute-done.9
  24.5 10.1 %collective-permute-done.18 = bf16[288,768]{1,0:T(8,128)(2,1)} collective-permute-done((bf16[288,768]{1,0:T(8,128)(2,1)S(1)}, bf16[288,768]{1,0:T(8,128)(2,1)}, u32[]{:S(2)}, u32[]{:S(2)}) %collective-permute-start.18) | collective-permute-done | bytes 442400 | tf_op jit(solution)/shard_map/ppermute | solution.py:92
  39.1 7.8 %collective-permute-done.26 = bf16[288,768]{1,0:T(8,128)(2,1)} collective-permute-done((bf16[288,768]{1,0:T(8,128)(2,1)}, bf16[288,768]{1,0:T(8,128)(2,1)}, u32[]{:S(2)}, u32[]{:S(2)}) %collective-permute-start.26) | collective-permute-done | bytes 442400 | tf_op jit(solution)/shard_map/ppermute | solution.py:92
  46.8 2.7 select_select_fusion
  51.9 7.3 %collective-permute-done = bf16[13,768]{1,0:T(8,128)(2,1)S(1)} collective-permute-done((bf16[13,768]{1,0:T(8,128)(2,1)S(1)}, bf16[13,768]{1,0:T(8,128)(2,1)S(1)}, u32[]{:S(2)}, u32[]{:S(2)}) %collective-permute-start) | collective-permute-done | bytes 20000 | tf_op jit(solution)/shard_map/ppermute | solution.py:230
  60.7 2.3 collective-permute-done.1
  64.3 2.7 collective-permute-done.2
  79.1 3.4 collective-permute-done.14.refs_6_
  83.5 2.5 collective-permute-start.16
  87.8 4.5 collective-permute-done.16
  93.1 54.7 %place.4 = bf16[4,288,768]{2,1,0:T(8,128)(2,1)} custom-call(s32[1]{0:T(128)} %bitcast.5.me_ref, bf16[288,768]{1,0:T(8,128)(2,1)} %copy-done.23, bf16[288,768]{1,0:T(8,128)(2,1)} %copy-done.27, bf16[288,768]{1,0:T(8,128)(2,1)} %copy-done.26, bf16[288,768]{1,0:T(8,128)(2,1)} %copy-done.28, bf16[288,768]{1,0:T(8,128)(2,1)} %copy-done.22, ...), custom_call_target="tpu_custom_call" | custom-call | bytes 3538944 | tf_op jit(solution)/shard_map/place/pallas_call | solution.py:139
  147.9 2.8 dynamic-slice_bitcast_fusion.3
  153.7 2.9 pad_maximum_fusion.u_ref
  156.6 2.0 collective-permute-done.21
  160.6 54.7 %place.5 = bf16[4,288,768]{2,1,0:T(8,128)(2,1)} custom-call(s32[1]{0:T(128)} %bitcast.5.me_ref, bf16[288,768]{1,0:T(8,128)(2,1)} %copy-done.23, bf16[288,768]{1,0:T(8,128)(2,1)} %copy-done.27, bf16[288,768]{1,0:T(8,128)(2,1)} %copy-done.26, bf16[288,768]{1,0:T(8,128)(2,1)} %copy-done.28, bf16[288,768]{1,0:T(8,128)(2,1)} %copy-done.22, ...), custom_call_target="tpu_custom_call" | custom-call | bytes 3538944 | tf_op jit(solution)/shard_map/place/pallas_call | solution.py:139
  216.7 2.4 maximum_select_fusion
  219.2 15.0 %attend.1 = (bf16[2,3,256,1152]{3,2,1,0:T(8,128)(2,1)}, bf16[2,3,256,384]{3,2,1,0:T(8,128)(2,1)S(1)}, f32[2,3,256,384]{3,2,1,0:T(8,128)S(1)}, f32[3,8,512]{2,1,0:T(8,128)S(1)}) custom-call(bf16[2,3,256,768]{3,2,1,0:T(8,128)(2,1)} %pad_maximum_fusion.u_ref, bf16[1152,768]{1,0:T(8,128)(2,1)S(1)} %bitcast.212, f32[1,1152]{1,0:T(1,128)S(1)} %copy-done.10), custom_call_target="tpu_custom_call" | custom-call | flops 7549747200 | bytes 12582912 | tf_op jit(solution)/shard_map/attend/pallas_call | solution.py:326
  247.2 6.1 collective-permute-done.28.refs_14_
  258.7 4.9 collective-permute-done.29
  265.0 54.7 %place.6 = bf16[4,288,768]{2,1,0:T(8,128)(2,1)} custom-call(s32[1]{0:T(128)} %bitcast.5.me_ref, bf16[288,768]{1,0:T(8,128)(2,1)} %copy-done.23, bf16[288,768]{1,0:T(8,128)(2,1)} %copy-done.27, bf16[288,768]{1,0:T(8,128)(2,1)} %copy-done.26, bf16[288,768]{1,0:T(8,128)(2,1)} %copy-done.28, bf16[288,768]{1,0:T(8,128)(2,1)} %copy-done.22, ...), custom_call_target="tpu_custom_call" | custom-call | bytes 3538944 | tf_op jit(solution)/shard_map/place/pallas_call | solution.py:139
  319.8 2.0 slice.384
  321.8 2.4 slice.381.w_ref
  325.3 54.7 %place.7 = bf16[4,288,768]{2,1,0:T(8,128)(2,1)} custom-call(s32[1]{0:T(128)} %bitcast.5.me_ref, bf16[288,768]{1,0:T(8,128)(2,1)} %copy-done.23, bf16[288,768]{1,0:T(8,128)(2,1)} %copy-done.27, bf16[288,768]{1,0:T(8,128)(2,1)} %copy-done.26, bf16[288,768]{1,0:T(8,128)(2,1)} %copy-done.28, bf16[288,768]{1,0:T(8,128)(2,1)} %copy-done.22, ...), custom_call_target="tpu_custom_call" | custom-call | bytes 3538944 | tf_op jit(solution)/shard_map/place/pallas_call | solution.py:139
  380.1 3.3 pad_maximum_fusion.1.h_ref
  383.3 5.6 hidden_units.2
  391.0 6.0 hidden_units.3
  400.0 3.0 fusion.21
  406.1 5.8 fusion.72
  414.8 4.1 convert_reduce_fusion.2
  419.2 2.9 collective-permute-done.32
  422.1 7.1 %convolution_convert_fusion = bf16[1536,768]{1,0:T(8,128)(2,1)S(1)} fusion(bf16[1536,1536]{1,0:T(8,128)(2,1)} %copy-done.45, bf16[768,768]{1,0:T(8,128)(2,1)} %collective-permute-done.32, bf16[768,768]{1,0:T(8,128)(2,1)} %get-tuple-element.60), kind=kOutput, calls=%fused_computation.5 | convolution fusion | flops 3629776896 | bytes 9437184 | tf_op jit(solution)/shard_map/dot_general | solution.py:37
  432.4 8.3 %convert_reduce_fusion = (f32[1536]{0:T(1024)}, bf16[1536,1536]{1,0:T(8,128)(2,1)S(1)}) fusion(bf16[1536,768]{1,0:T(8,128)(2,1)S(1)} %copy-done.15, bf16[1536,768]{1,0:T(8,128)(2,1)S(1)} %copy-done.13, bf16[1152,768]{1,0:T(8,128)(2,1)S(1)} %bitcast.249, bf16[384,768]{1,0:T(8,128)(2,1)S(1)} %copy-done.47, bf16[768,768]{1,0:T(8,128)(2,1)} %collective-permute-done.32, ...), kind=kOutput, calls=%fused_computation.1 | convolution fusion | flops 3652188672 | bytes 14161920 | tf_op jit(solution)/shard_map/dot_general | solution.py:37
  442.7 5.8 convolution_convert_fusion.1
  454.2 3.9 collective-permute-done.56
  465.8 6.6 %collective-permute-done.59 = bf16[288,768]{1,0:T(8,128)(2,1)S(1)} collective-permute-done((bf16[288,768]{1,0:T(8,128)(2,1)S(1)}, bf16[288,768]{1,0:T(8,128)(2,1)S(1)}, u32[]{:S(2)}, u32[]{:S(2)}) %collective-permute-start.59) | collective-permute-done | bytes 442400 | tf_op jit(solution)/shard_map/ppermute | solution.py:92
  473.9 2.3 collective-permute-start.60
  476.2 3.3 multiply_reduce_fusion
  479.5 2.2 convert_reduce_fusion.3
  482.8 3.4 collective-permute-start.54
  495.1 2.0 add_convert_fusion.4
  501.6 2.0 add_convert_fusion.1
  507.3 23.9 %attend_back.1 = (bf16[2,3,256,1152]{3,2,1,0:T(8,128)(2,1)}, f32[1,1152]{1,0:T(1,128)S(1)}) custom-call(bf16[2,3,256,1152]{3,2,1,0:T(8,128)(2,1)} %get-tuple-element.28.qkv_ref, bf16[2,3,256,768]{3,2,1,0:T(8,128)(2,1)S(1)} %bitcast.211, bf16[768,384]{1,0:T(8,128)(2,1)S(1)} %bitcast.209, f32[2,3,256,384]{3,2,1,0:T(8,128)S(1)} %copy-done.17, ...), custom_call_target="tpu_custom_call" | custom-call | flops 12985565184 | bytes 12582912 | tf_op jit(solution)/shard_map/attend_back/pallas_call | solution.py:395
  531.2 5.3 fusion.1
  537.8 3.2 convolution_convert_fusion.3
  544.9 5.8 collective-permute-done.37
  552.2 3.2 collective-permute-done.44
  555.7 2.6 collective-permute-done.46
  559.5 5.4 collective-permute-done.40
  570.2 2.6 collective-permute-done.47
  572.8 2.8 collective-permute-done.45
  575.7 6.0 collective-permute-start.48
  584.3 4.7 collective-permute-done.48
  591.8 2.6 corrupt_back.1
  596.8 3.2 collective-permute-done.69
  600.8 3.3 collective-permute-done.70
  604.2 3.2 collective-permute-start.71
  609.4 3.6 collective-permute-start.72
  613.1 2.5 multiply_reduce_fusion.5
  619.0 2.2 collective-permute-start.64
  623.2 2.1 collective-permute-start.65
  631.7 3.5 collective-permute-start.67
  641.3 3.9 fusion.59
  (414 shorter events, 145.5 us)
Async XLA Ops:
  3.3 14.3 %collective-permute-start.10 = (bf16[288,768]{1,0:T(8,128)(2,1)S(1)}, bf16[288,768]{1,0:T(8,128)(2,1)S(1)}, u32[]{:S(2)}, u32[]{:S(2)}) collective-permute-start(bf16[288,768]{1,0:T(8,128)(2,1)S(1)} %maximum_select_fusion.2.refs_0_), channel_id=1, source_target_pairs={{0,8},{2,10},{4,12},{6,14},{8,16},{10,18},{12,20},{14,22},{16,24},... | collective-permute-start | bytes 1327112 | tf_op jit(solution)/shard_map/ppermute | solution.py:92
  8.2 13.5 %collective-permute-start.9 = (bf16[288,768]{1,0:T(8,128)(2,1)S(1)}, bf16[288,768]{1,0:T(8,128)(2,1)S(1)}, u32[]{:S(2)}, u32[]{:S(2)}) collective-permute-start(bf16[288,768]{1,0:T(8,128)(2,1)S(1)} %maximum_select_fusion.2.refs_0_), channel_id=1, source_target_pairs={{8,0},{10,2},{12,4},{14,6},{16,8},{18,10},{20,12},{22,14},{24,16},... | collective-permute-start | bytes 1327112 | tf_op jit(solution)/shard_map/ppermute | solution.py:92
  17.6 5.4 collective-permute-start.11
  21.8 12.9 %collective-permute-start.18 = (bf16[288,768]{1,0:T(8,128)(2,1)S(1)}, bf16[288,768]{1,0:T(8,128)(2,1)}, u32[]{:S(2)}, u32[]{:S(2)}) collective-permute-start(bf16[288,768]{1,0:T(8,128)(2,1)S(1)} %collective-permute-done.9), channel_id=1, source_target_pairs={{8,0},{10,2},{12,4},{14,6},{16,8},{18,10},{20,12},{22,14},{9,1},{1... | collective-permute-start | bytes 1327112 | tf_op jit(solution)/shard_map/ppermute | solution.py:92
  23.1 16.0 %collective-permute-start.12 = (bf16[288,768]{1,0:T(8,128)(2,1)S(1)}, bf16[288,768]{1,0:T(8,128)(2,1)}, u32[]{:S(2)}, u32[]{:S(2)}) collective-permute-start(bf16[288,768]{1,0:T(8,128)(2,1)S(1)} %collective-permute-done.11), channel_id=1, source_target_pairs={{16,24},{18,26},{20,28},{22,30},{17,25},{19,27},{21,29},{23,31}} | collective-permute-start | bytes 1327112 | tf_op jit(solution)/shard_map/ppermute | solution.py:92
  34.6 12.2 %collective-permute-start.26 = (bf16[288,768]{1,0:T(8,128)(2,1)}, bf16[288,768]{1,0:T(8,128)(2,1)}, u32[]{:S(2)}, u32[]{:S(2)}) collective-permute-start(bf16[288,768]{1,0:T(8,128)(2,1)} %collective-permute-done.18), channel_id=1, source_target_pairs={{8,0},{10,2},{12,4},{14,6},{9,1},{11,3},{13,5},{15,7}} | collective-permute-start | bytes 1327112 | tf_op jit(solution)/shard_map/ppermute | solution.py:92
  35.9 36.5 %collective-permute-start.6 = (bf16[288,768]{1,0:T(8,128)(2,1)S(1)}, bf16[288,768]{1,0:T(8,128)(2,1)S(1)}, u32[]{:S(2)}, u32[]{:S(2)}) collective-permute-start(bf16[288,768]{1,0:T(8,128)(2,1)S(1)} %maximum_select_fusion.2.refs_0_), channel_id=1, source_target_pairs={{0,4},{2,6},{4,0},{6,2},{8,12},{10,14},{12,8},{14,10},{16,20},{18,... | collective-permute-start | bytes 1327112 | tf_op jit(solution)/shard_map/ppermute | solution.py:92
  37.5 31.2 %collective-permute-start.5 = (bf16[288,768]{1,0:T(8,128)(2,1)S(1)}, bf16[288,768]{1,0:T(8,128)(2,1)S(1)}, u32[]{:S(2)}, u32[]{:S(2)}) collective-permute-start(bf16[288,768]{1,0:T(8,128)(2,1)S(1)} %maximum_select_fusion.2.refs_0_), channel_id=1, source_target_pairs={{0,2},{2,0},{4,6},{6,4},{8,10},{10,8},{12,14},{14,12},{16,18},{18,... | collective-permute-start | bytes 1327112 | tf_op jit(solution)/shard_map/ppermute | solution.py:92
  49.6 26.1 %collective-permute-start.13 = (bf16[288,768]{1,0:T(8,128)(2,1)S(1)}, bf16[288,768]{1,0:T(8,128)(2,1)}, u32[]{:S(2)}, u32[]{:S(2)}) collective-permute-start(bf16[288,768]{1,0:T(8,128)(2,1)S(1)} %get-tuple-element.106.refs_4_), channel_id=1, source_target_pairs={{0,2},{2,0},{4,6},{6,4},{8,10},{10,8},{12,14},{14,12},{16,18},{18,... | collective-permute-start | bytes 1327112 | tf_op jit(solution)/shard_map/ppermute | solution.py:92
  51.3 7.9 %collective-permute-start = (bf16[13,768]{1,0:T(8,128)(2,1)S(1)}, bf16[13,768]{1,0:T(8,128)(2,1)S(1)}, u32[]{:S(2)}, u32[]{:S(2)}) collective-permute-start(bf16[13,768]{1,0:T(8,128)(2,1)S(1)} %reshape.266), channel_id=1, source_target_pairs={{0,2},{2,0},{4,6},{6,4},{8,10},{10,8},{12,14},{14,12},{16,18},{18,... | collective-permute-start | bytes 59912 | tf_op jit(solution)/shard_map/ppermute | solution.py:230
  67.0 4.8 collective-permute-start.3
  69.4 8.7 %collective-permute-start.7 = (bf16[144,768]{1,0:T(8,128)(2,1)}, bf16[144,768]{1,0:T(8,128)(2,1)}, u32[]{:S(2)}, u32[]{:S(2)}) collective-permute-start(bf16[144,768]{1,0:T(8,128)(2,1)} %slice.364), channel_id=1, source_target_pairs={{0,4},{2,6},{4,0},{6,2},{8,12},{10,14},{12,8},{14,10},{16,20},{18,... | collective-permute-start | bytes 663560 | tf_op jit(solution)/shard_map/ppermute | solution.py:92
  69.9 12.6 %collective-permute-start.14 = (bf16[288,768]{1,0:T(8,128)(2,1)S(1)}, bf16[288,768]{1,0:T(8,128)(2,1)}, u32[]{:S(2)}, u32[]{:S(2)}) collective-permute-start(bf16[288,768]{1,0:T(8,128)(2,1)S(1)} %get-tuple-element.106.refs_4_), channel_id=1, source_target_pairs={{0,4},{2,6},{4,0},{6,2},{8,12},{10,14},{12,8},{14,10},{16,20},{18,... | collective-permute-start | bytes 1327112 | tf_op jit(solution)/shard_map/ppermute | solution.py:92
  73.1 12.9 %collective-permute-start.8 = (bf16[144,768]{1,0:T(8,128)(2,1)}, bf16[144,768]{1,0:T(8,128)(2,1)}, u32[]{:S(2)}, u32[]{:S(2)}) collective-permute-start(bf16[144,768]{1,0:T(8,128)(2,1)} %slice.365), channel_id=1, source_target_pairs={{0,2},{2,0},{4,6},{6,4},{8,10},{10,8},{12,14},{14,12},{16,18},{18,... | collective-permute-start | bytes 663560 | tf_op jit(solution)/shard_map/ppermute | solution.py:92
  75.5 78.2 %collective-permute-start.4 = (bf16[3,256,768]{2,1,0:T(8,128)(2,1)S(1)}, bf16[3,256,768]{2,1,0:T(8,128)(2,1)}, u32[]{:S(2)}, u32[]{:S(2)}) collective-permute-start(bf16[3,256,768]{2,1,0:T(8,128)(2,1)S(1)} %corrupt.1), channel_id=1, source_target_pairs={{0,1},{1,0},{2,3},{3,2},{4,5},{5,4},{6,7},{7,6},{8,9},{9,8},{10,11... | collective-permute-start | bytes 3538952 | tf_op jit(solution)/shard_map/ppermute | solution.py:46
  76.6 11.2 %collective-permute-start.15 = (bf16[144,768]{1,0:T(8,128)(2,1)S(1)}, bf16[144,768]{1,0:T(8,128)(2,1)S(1)}, u32[]{:S(2)}, u32[]{:S(2)}) collective-permute-start(bf16[144,768]{1,0:T(8,128)(2,1)S(1)} %slice.366), channel_id=1, source_target_pairs={{0,4},{2,6},{4,0},{6,2},{8,12},{10,14},{12,8},{14,10},{16,20},{18,... | collective-permute-start | bytes 663560 | tf_op jit(solution)/shard_map/ppermute | solution.py:92
  83.5 8.9 %collective-permute-start.16 = (bf16[144,768]{1,0:T(8,128)(2,1)S(1)}, bf16[144,768]{1,0:T(8,128)(2,1)S(1)}, u32[]{:S(2)}, u32[]{:S(2)}) collective-permute-start(bf16[144,768]{1,0:T(8,128)(2,1)S(1)} %slice.367), channel_id=1, source_target_pairs={{0,2},{2,0},{4,6},{6,4},{8,10},{10,8},{12,14},{14,12},{16,18},{18,... | collective-permute-start | bytes 663560 | tf_op jit(solution)/shard_map/ppermute | solution.py:92
  86.9 65.2 %collective-permute-start.20 = (bf16[288,768]{1,0:T(8,128)(2,1)S(1)}, bf16[288,768]{1,0:T(8,128)(2,1)S(1)}, u32[]{:S(2)}, u32[]{:S(2)}) collective-permute-start(bf16[288,768]{1,0:T(8,128)(2,1)S(1)} %copy-done.30), channel_id=1, source_target_pairs={{0,4},{2,6},{4,0},{6,2},{8,12},{10,14},{12,8},{14,10},{16,20},{18,... | collective-permute-start | bytes 1327112 | tf_op jit(solution)/shard_map/ppermute | solution.py:92
  87.8 62.9 %collective-permute-start.19 = (bf16[288,768]{1,0:T(8,128)(2,1)S(1)}, bf16[288,768]{1,0:T(8,128)(2,1)S(1)}, u32[]{:S(2)}, u32[]{:S(2)}) collective-permute-start(bf16[288,768]{1,0:T(8,128)(2,1)S(1)} %copy-done.30), channel_id=1, source_target_pairs={{0,2},{2,0},{4,6},{6,4},{8,10},{10,8},{12,14},{14,12},{16,18},{18,... | collective-permute-start | bytes 1327112 | tf_op jit(solution)/shard_map/ppermute | solution.py:92
  150.6 66.1 %collective-permute-start.17 = (bf16[3,2,96,768]{3,2,1,0:T(8,128)(2,1)}, bf16[3,2,96,768]{3,2,1,0:T(8,128)(2,1)}, u32[]{:S(2)}, u32[]{:S(2)}) collective-permute-start(bf16[3,2,96,768]{3,2,1,0:T(8,128)(2,1)} %get-tuple-element.103), channel_id=1, source_target_pairs={{0,1},{1,0},{2,3},{3,2},{4,5},{5,4},{6,7},{7,6},{8,9},{9,8},{10,11... | collective-permute-start | bytes 2654216 | tf_op jit(solution)/shard_map/ppermute | solution.py:46
  150.7 7.9 %collective-permute-start.21 = (bf16[144,768]{1,0:T(8,128)(2,1)S(1)}, bf16[144,768]{1,0:T(8,128)(2,1)S(1)}, u32[]{:S(2)}, u32[]{:S(2)}) collective-permute-start(bf16[144,768]{1,0:T(8,128)(2,1)S(1)} %slice.370), channel_id=1, source_target_pairs={{0,4},{2,6},{4,0},{6,2},{8,12},{10,14},{12,8},{14,10},{16,20},{18,... | collective-permute-start | bytes 663560 | tf_op jit(solution)/shard_map/ppermute | solution.py:92
  152.1 7.6 %collective-permute-start.22 = (bf16[144,768]{1,0:T(8,128)(2,1)S(1)}, bf16[144,768]{1,0:T(8,128)(2,1)S(1)}, u32[]{:S(2)}, u32[]{:S(2)}) collective-permute-start(bf16[144,768]{1,0:T(8,128)(2,1)S(1)} %slice.371), channel_id=1, source_target_pairs={{0,2},{2,0},{4,6},{6,4},{8,10},{10,8},{12,14},{14,12},{16,18},{18,... | collective-permute-start | bytes 663560 | tf_op jit(solution)/shard_map/ppermute | solution.py:92
  216.6 20.7 %collective-permute-start.24 = (bf16[768,384]{1,0:T(8,128)(2,1)S(1)}, bf16[768,384]{1,0:T(8,128)(2,1)S(1)}, u32[]{:S(2)}, u32[]{:S(2)}) collective-permute-start(bf16[768,384]{1,0:T(8,128)(2,1)S(1)} %bitcast.207), channel_id=1, source_target_pairs={{0,1},{1,0},{2,3},{3,2},{4,5},{5,4},{6,7},{7,6},{8,9},{9,8},{10,11... | collective-permute-start | bytes 1769480 | tf_op jit(solution)/shard_map/ppermute | solution.py:46
  240.4 139.7 %collective-permute-start.25 = (bf16[768,768]{1,0:T(8,128)(2,1)}, bf16[768,768]{1,0:T(8,128)(2,1)}, u32[]{:S(2)}, u32[]{:S(2)}) collective-permute-start(bf16[768,768]{1,0:T(8,128)(2,1)} %fusion.17), channel_id=1, source_target_pairs={{0,1},{1,0},{2,3},{3,2},{4,5},{5,4},{6,7},{7,6},{8,9},{9,8},{10,11... | collective-permute-start | bytes 3538952 | tf_op jit(solution)/shard_map/ppermute | solution.py:46
  240.4 12.9 %collective-permute-start.28 = (bf16[288,768]{1,0:T(8,128)(2,1)}, bf16[288,768]{1,0:T(8,128)(2,1)}, u32[]{:S(2)}, u32[]{:S(2)}) collective-permute-start(bf16[288,768]{1,0:T(8,128)(2,1)} %get-tuple-element.104.refs_12_), channel_id=1, source_target_pairs={{0,4},{2,6},{4,0},{6,2},{8,12},{10,14},{12,8},{14,10},{16,20},{18,... | collective-permute-start | bytes 1327112 | tf_op jit(solution)/shard_map/ppermute | solution.py:92
  241.8 14.1 %collective-permute-start.27 = (bf16[288,768]{1,0:T(8,128)(2,1)}, bf16[288,768]{1,0:T(8,128)(2,1)}, u32[]{:S(2)}, u32[]{:S(2)}) collective-permute-start(bf16[288,768]{1,0:T(8,128)(2,1)} %get-tuple-element.104.refs_12_), channel_id=1, source_target_pairs={{0,2},{2,0},{4,6},{6,4},{8,10},{10,8},{12,14},{14,12},{16,18},{18,... | collective-permute-start | bytes 1327112 | tf_op jit(solution)/shard_map/ppermute | solution.py:92
  254.3 10.0 %collective-permute-start.30 = (bf16[144,768]{1,0:T(8,128)(2,1)S(1)}, bf16[144,768]{1,0:T(8,128)(2,1)S(1)}, u32[]{:S(2)}, u32[]{:S(2)}) collective-permute-start(bf16[144,768]{1,0:T(8,128)(2,1)S(1)} %slice.380), channel_id=1, source_target_pairs={{0,2},{2,0},{4,6},{6,4},{8,10},{10,8},{12,14},{14,12},{16,18},{18,... | collective-permute-start | bytes 663560 | tf_op jit(solution)/shard_map/ppermute | solution.py:92
  256.8 6.8 %collective-permute-start.29 = (bf16[144,768]{1,0:T(8,128)(2,1)S(1)}, bf16[144,768]{1,0:T(8,128)(2,1)S(1)}, u32[]{:S(2)}, u32[]{:S(2)}) collective-permute-start(bf16[144,768]{1,0:T(8,128)(2,1)S(1)} %slice.379), channel_id=1, source_target_pairs={{0,4},{2,6},{4,0},{6,2},{8,12},{10,14},{12,8},{14,10},{16,20},{18,... | collective-permute-start | bytes 663560 | tf_op jit(solution)/shard_map/ppermute | solution.py:92
  449.8 8.3 %collective-permute-start.56 = (bf16[144,768]{1,0:T(8,128)(2,1)S(1)}, bf16[144,768]{1,0:T(8,128)(2,1)S(1)}, u32[]{:S(2)}, u32[]{:S(2)}) collective-permute-start(bf16[144,768]{1,0:T(8,128)(2,1)S(1)} %get-tuple-element.98), channel_id=1, source_target_pairs={{0,4},{2,6},{4,0},{6,2},{8,12},{10,14},{12,8},{14,10},{16,20},{18,... | collective-permute-start | bytes 663560 | tf_op jit(solution)/shard_map/ppermute | solution.py:92
  450.4 8.3 %collective-permute-start.58 = (bf16[144,768]{1,0:T(8,128)(2,1)S(1)}, bf16[144,768]{1,0:T(8,128)(2,1)S(1)}, u32[]{:S(2)}, u32[]{:S(2)}) collective-permute-start(bf16[144,768]{1,0:T(8,128)(2,1)S(1)} %get-tuple-element.100), channel_id=1, source_target_pairs={{0,2},{2,0},{4,6},{6,4},{8,10},{10,8},{12,14},{14,12},{16,18},{18,... | collective-permute-start | bytes 663560 | tf_op jit(solution)/shard_map/ppermute | solution.py:92
  451.9 11.0 %collective-permute-start.50 = (bf16[144,768]{1,0:T(8,128)(2,1)S(1)}, bf16[144,768]{1,0:T(8,128)(2,1)S(1)}, u32[]{:S(2)}, u32[]{:S(2)}) collective-permute-start(bf16[144,768]{1,0:T(8,128)(2,1)S(1)} %get-tuple-element.92), channel_id=1, source_target_pairs={{0,4},{2,6},{4,0},{6,2},{8,12},{10,14},{12,8},{14,10},{16,20},{18,... | collective-permute-start | bytes 663560 | tf_op jit(solution)/shard_map/ppermute | solution.py:92
  452.7 10.8 %collective-permute-start.52 = (bf16[144,768]{1,0:T(8,128)(2,1)S(1)}, bf16[144,768]{1,0:T(8,128)(2,1)S(1)}, u32[]{:S(2)}, u32[]{:S(2)}) collective-permute-start(bf16[144,768]{1,0:T(8,128)(2,1)S(1)} %get-tuple-element.94), channel_id=1, source_target_pairs={{0,2},{2,0},{4,6},{6,4},{8,10},{10,8},{12,14},{14,12},{16,18},{18,... | collective-permute-start | bytes 663560 | tf_op jit(solution)/shard_map/ppermute | solution.py:92
  454.2 22.0 %collective-permute-start.33 = (bf16[768,768]{1,0:T(8,128)(2,1)S(1)}, bf16[768,768]{1,0:T(8,128)(2,1)S(1)}, u32[]{:S(2)}, u32[]{:S(2)}) collective-permute-start(bf16[768,768]{1,0:T(8,128)(2,1)S(1)} %fusion.24), channel_id=1, source_target_pairs={{0,1},{1,0},{2,3},{3,2},{4,5},{5,4},{6,7},{7,6},{8,9},{9,8},{10,11... | collective-permute-start | bytes 3538952 | tf_op jit(solution)/shard_map/ppermute | solution.py:46
  458.9 13.5 %collective-permute-start.59 = (bf16[288,768]{1,0:T(8,128)(2,1)S(1)}, bf16[288,768]{1,0:T(8,128)(2,1)S(1)}, u32[]{:S(2)}, u32[]{:S(2)}) collective-permute-start(bf16[288,768]{1,0:T(8,128)(2,1)S(1)} %pad_maximum_fusion.26), channel_id=1, source_target_pairs={{0,4},{2,6},{4,0},{6,2},{8,12},{10,14},{12,8},{14,10},{16,20},{18,... | collective-permute-start | bytes 1327112 | tf_op jit(solution)/shard_map/ppermute | solution.py:92
  460.5 13.2 %collective-permute-start.57 = (bf16[288,768]{1,0:T(8,128)(2,1)S(1)}, bf16[288,768]{1,0:T(8,128)(2,1)S(1)}, u32[]{:S(2)}, u32[]{:S(2)}) collective-permute-start(bf16[288,768]{1,0:T(8,128)(2,1)S(1)} %pad_maximum_fusion.25), channel_id=1, source_target_pairs={{0,2},{2,0},{4,6},{6,4},{8,10},{10,8},{12,14},{14,12},{16,18},{18,... | collective-permute-start | bytes 1327112 | tf_op jit(solution)/shard_map/ppermute | solution.py:92
  463.6 18.3 %collective-permute-start.53 = (bf16[288,768]{1,0:T(8,128)(2,1)S(1)}, bf16[288,768]{1,0:T(8,128)(2,1)S(1)}, u32[]{:S(2)}, u32[]{:S(2)}) collective-permute-start(bf16[288,768]{1,0:T(8,128)(2,1)S(1)} %pad_maximum_fusion.24), channel_id=1, source_target_pairs={{0,4},{2,6},{4,0},{6,2},{8,12},{10,14},{12,8},{14,10},{16,20},{18,... | collective-permute-start | bytes 1327112 | tf_op jit(solution)/shard_map/ppermute | solution.py:92
  465.2 16.7 %collective-permute-start.51 = (bf16[288,768]{1,0:T(8,128)(2,1)S(1)}, bf16[288,768]{1,0:T(8,128)(2,1)S(1)}, u32[]{:S(2)}, u32[]{:S(2)}) collective-permute-start(bf16[288,768]{1,0:T(8,128)(2,1)S(1)} %pad_maximum_fusion.23), channel_id=1, source_target_pairs={{0,2},{2,0},{4,6},{6,4},{8,10},{10,8},{12,14},{14,12},{16,18},{18,... | collective-permute-start | bytes 1327112 | tf_op jit(solution)/shard_map/ppermute | solution.py:92
  473.9 12.4 %collective-permute-start.60 = (bf16[288,768]{1,0:T(8,128)(2,1)S(1)}, bf16[288,768]{1,0:T(8,128)(2,1)S(1)}, u32[]{:S(2)}, u32[]{:S(2)}) collective-permute-start(bf16[288,768]{1,0:T(8,128)(2,1)S(1)} %fusion.28), channel_id=1, source_target_pairs={{0,8},{2,10},{4,12},{6,14},{1,9},{3,11},{5,13},{7,15}} | collective-permute-start | bytes 1327112 | tf_op jit(solution)/shard_map/ppermute | solution.py:92
  481.8 23.7 %collective-permute-start.34 = (bf16[768,768]{1,0:T(8,128)(2,1)}, bf16[768,768]{1,0:T(8,128)(2,1)}, u32[]{:S(2)}, u32[]{:S(2)}) collective-permute-start(bf16[768,768]{1,0:T(8,128)(2,1)} %get-tuple-element.63), channel_id=1, source_target_pairs={{0,1},{1,0},{2,3},{3,2},{4,5},{5,4},{6,7},{7,6},{8,9},{9,8},{10,11... | collective-permute-start | bytes 3538952 | tf_op jit(solution)/shard_map/ppermute | solution.py:46
  482.8 12.3 %collective-permute-start.54 = (bf16[288,768]{1,0:T(8,128)(2,1)}, bf16[288,768]{1,0:T(8,128)(2,1)}, u32[]{:S(2)}, u32[]{:S(2)}) collective-permute-start(bf16[288,768]{1,0:T(8,128)(2,1)} %fusion.30), channel_id=1, source_target_pairs={{0,8},{2,10},{4,12},{6,14},{24,16},{26,18},{28,20},{30,22},{1,9},{... | collective-permute-start | bytes 1327112 | tf_op jit(solution)/shard_map/ppermute | solution.py:92
  487.1 14.5 %collective-permute-start.61 = (bf16[288,768]{1,0:T(8,128)(2,1)}, bf16[288,768]{1,0:T(8,128)(2,1)}, u32[]{:S(2)}, u32[]{:S(2)}) collective-permute-start(bf16[288,768]{1,0:T(8,128)(2,1)} %add_convert_fusion.2), channel_id=1, source_target_pairs={{8,16},{10,18},{12,20},{14,22},{9,17},{11,19},{13,21},{15,23}} | collective-permute-start | bytes 1327112 | tf_op jit(solution)/shard_map/ppermute | solution.py:92
  497.1 116.0 %collective-permute-start.55 = (bf16[288,768]{1,0:T(8,128)(2,1)}, bf16[288,768]{1,0:T(8,128)(2,1)}, u32[]{:S(2)}, u32[]{:S(2)}) collective-permute-start(bf16[288,768]{1,0:T(8,128)(2,1)} %add_convert_fusion.4), channel_id=1, source_target_pairs={{8,16},{10,18},{12,20},{14,22},{9,17},{11,19},{13,21},{15,23}} | collective-permute-start | bytes 1327112 | tf_op jit(solution)/shard_map/ppermute | solution.py:92
  503.6 109.4 %collective-permute-start.62 = (bf16[288,768]{1,0:T(8,128)(2,1)}, bf16[288,768]{1,0:T(8,128)(2,1)}, u32[]{:S(2)}, u32[]{:S(2)}) collective-permute-start(bf16[288,768]{1,0:T(8,128)(2,1)} %add_convert_fusion.1), channel_id=1, source_target_pairs={{16,24},{18,26},{20,28},{22,30},{17,25},{19,27},{21,29},{23,31}} | collective-permute-start | bytes 1327112 | tf_op jit(solution)/shard_map/ppermute | solution.py:92
  536.6 5.2 collective-permute-start.36
  542.2 8.4 %collective-permute-start.37 = (bf16[144,768]{1,0:T(8,128)(2,1)S(1)}, bf16[144,768]{1,0:T(8,128)(2,1)S(1)}, u32[]{:S(2)}, u32[]{:S(2)}) collective-permute-start(bf16[144,768]{1,0:T(8,128)(2,1)S(1)} %get-tuple-element.78), channel_id=1, source_target_pairs={{0,4},{2,6},{4,0},{6,2},{8,12},{10,14},{12,8},{14,10},{16,20},{18,... | collective-permute-start | bytes 663560 | tf_op jit(solution)/shard_map/ppermute | solution.py:92
  543.2 7.7 %collective-permute-start.39 = (bf16[144,768]{1,0:T(8,128)(2,1)S(1)}, bf16[144,768]{1,0:T(8,128)(2,1)S(1)}, u32[]{:S(2)}, u32[]{:S(2)}) collective-permute-start(bf16[144,768]{1,0:T(8,128)(2,1)S(1)} %get-tuple-element.80), channel_id=1, source_target_pairs={{0,2},{2,0},{4,6},{6,4},{8,10},{10,8},{12,14},{14,12},{16,18},{18,... | collective-permute-start | bytes 663560 | tf_op jit(solution)/shard_map/ppermute | solution.py:92
  543.8 11.6 %collective-permute-start.44 = (bf16[144,768]{1,0:T(8,128)(2,1)S(1)}, bf16[144,768]{1,0:T(8,128)(2,1)S(1)}, u32[]{:S(2)}, u32[]{:S(2)}) collective-permute-start(bf16[144,768]{1,0:T(8,128)(2,1)S(1)} %get-tuple-element.86), channel_id=1, source_target_pairs={{0,4},{2,6},{4,0},{6,2},{8,12},{10,14},{12,8},{14,10},{16,20},{18,... | collective-permute-start | bytes 663560 | tf_op jit(solution)/shard_map/ppermute | solution.py:92
  550.6 7.6 %collective-permute-start.46 = (bf16[144,768]{1,0:T(8,128)(2,1)S(1)}, bf16[144,768]{1,0:T(8,128)(2,1)S(1)}, u32[]{:S(2)}, u32[]{:S(2)}) collective-permute-start(bf16[144,768]{1,0:T(8,128)(2,1)S(1)} %get-tuple-element.88), channel_id=1, source_target_pairs={{0,2},{2,0},{4,6},{6,4},{8,10},{10,8},{12,14},{14,12},{16,18},{18,... | collective-permute-start | bytes 663560 | tf_op jit(solution)/shard_map/ppermute | solution.py:92
  551.1 13.8 %collective-permute-start.40 = (bf16[288,768]{1,0:T(8,128)(2,1)S(1)}, bf16[288,768]{1,0:T(8,128)(2,1)S(1)}, u32[]{:S(2)}, u32[]{:S(2)}) collective-permute-start(bf16[288,768]{1,0:T(8,128)(2,1)S(1)} %pad_maximum_fusion.20), channel_id=1, source_target_pairs={{0,4},{2,6},{4,0},{6,2},{8,12},{10,14},{12,8},{14,10},{16,20},{18,... | collective-permute-start | bytes 1327112 | tf_op jit(solution)/shard_map/ppermute | solution.py:92
  555.4 12.3 %collective-permute-start.38 = (bf16[288,768]{1,0:T(8,128)(2,1)S(1)}, bf16[288,768]{1,0:T(8,128)(2,1)S(1)}, u32[]{:S(2)}, u32[]{:S(2)}) collective-permute-start(bf16[288,768]{1,0:T(8,128)(2,1)S(1)} %pad_maximum_fusion.19), channel_id=1, source_target_pairs={{0,2},{2,0},{4,6},{6,4},{8,10},{10,8},{12,14},{14,12},{16,18},{18,... | collective-permute-start | bytes 1327112 | tf_op jit(solution)/shard_map/ppermute | solution.py:92
  558.4 14.3 %collective-permute-start.47 = (bf16[288,768]{1,0:T(8,128)(2,1)S(1)}, bf16[288,768]{1,0:T(8,128)(2,1)S(1)}, u32[]{:S(2)}, u32[]{:S(2)}) collective-permute-start(bf16[288,768]{1,0:T(8,128)(2,1)S(1)} %pad_maximum_fusion.22), channel_id=1, source_target_pairs={{0,4},{2,6},{4,0},{6,2},{8,12},{10,14},{12,8},{14,10},{16,20},{18,... | collective-permute-start | bytes 1327112 | tf_op jit(solution)/shard_map/ppermute | solution.py:92
  564.9 10.7 %collective-permute-start.45 = (bf16[288,768]{1,0:T(8,128)(2,1)S(1)}, bf16[288,768]{1,0:T(8,128)(2,1)S(1)}, u32[]{:S(2)}, u32[]{:S(2)}) collective-permute-start(bf16[288,768]{1,0:T(8,128)(2,1)S(1)} %pad_maximum_fusion.21), channel_id=1, source_target_pairs={{0,2},{2,0},{4,6},{6,4},{8,10},{10,8},{12,14},{14,12},{16,18},{18,... | collective-permute-start | bytes 1327112 | tf_op jit(solution)/shard_map/ppermute | solution.py:92
  567.8 13.9 %collective-permute-start.41 = (bf16[288,768]{1,0:T(8,128)(2,1)S(1)}, bf16[288,768]{1,0:T(8,128)(2,1)S(1)}, u32[]{:S(2)}, u32[]{:S(2)}) collective-permute-start(bf16[288,768]{1,0:T(8,128)(2,1)S(1)} %fusion.34), channel_id=1, source_target_pairs={{24,16},{26,18},{28,20},{30,22},{25,17},{27,19},{29,21},{31,23}} | collective-permute-start | bytes 1327112 | tf_op jit(solution)/shard_map/ppermute | solution.py:92
  572.8 19.0 %collective-permute-start.35 = (bf16[768,768]{1,0:T(8,128)(2,1)S(1)}, bf16[768,768]{1,0:T(8,128)(2,1)S(1)}, u32[]{:S(2)}, u32[]{:S(2)}) collective-permute-start(bf16[768,768]{1,0:T(8,128)(2,1)S(1)} %convolution_convert_fusion.2), channel_id=1, source_target_pairs={{0,1},{1,0},{2,3},{3,2},{4,5},{5,4},{6,7},{7,6},{8,9},{9,8},{10,11... | collective-permute-start | bytes 3538952 | tf_op jit(solution)/shard_map/ppermute | solution.py:46
  575.7 13.3 %collective-permute-start.48 = (bf16[288,768]{1,0:T(8,128)(2,1)S(1)}, bf16[288,768]{1,0:T(8,128)(2,1)S(1)}, u32[]{:S(2)}, u32[]{:S(2)}) collective-permute-start(bf16[288,768]{1,0:T(8,128)(2,1)S(1)} %fusion.32), channel_id=1, source_target_pairs={{24,16},{26,18},{28,20},{30,22},{0,8},{2,10},{4,12},{6,14},{25,17}... | collective-permute-start | bytes 1327112 | tf_op jit(solution)/shard_map/ppermute | solution.py:92
  581.8 8.2 %collective-permute-start.42 = (bf16[288,768]{1,0:T(8,128)(2,1)S(1)}, bf16[288,768]{1,0:T(8,128)(2,1)S(1)}, u32[]{:S(2)}, u32[]{:S(2)}) collective-permute-start(bf16[288,768]{1,0:T(8,128)(2,1)S(1)} %add_convert_fusion.9), channel_id=1, source_target_pairs={{16,8},{18,10},{20,12},{22,14},{17,9},{19,11},{21,13},{23,15}} | collective-permute-start | bytes 1327112 | tf_op jit(solution)/shard_map/ppermute | solution.py:92
  589.2 23.9 %collective-permute-start.49 = (bf16[288,768]{1,0:T(8,128)(2,1)S(1)}, bf16[288,768]{1,0:T(8,128)(2,1)S(1)}, u32[]{:S(2)}, u32[]{:S(2)}) collective-permute-start(bf16[288,768]{1,0:T(8,128)(2,1)S(1)} %add_convert_fusion.6), channel_id=1, source_target_pairs={{16,8},{18,10},{20,12},{22,14},{17,9},{19,11},{21,13},{23,15}} | collective-permute-start | bytes 1327112 | tf_op jit(solution)/shard_map/ppermute | solution.py:92
  590.1 22.9 %collective-permute-start.43 = (bf16[288,768]{1,0:T(8,128)(2,1)S(1)}, bf16[288,768]{1,0:T(8,128)(2,1)S(1)}, u32[]{:S(2)}, u32[]{:S(2)}) collective-permute-start(bf16[288,768]{1,0:T(8,128)(2,1)S(1)} %add_convert_fusion.8), channel_id=1, source_target_pairs={{8,0},{10,2},{12,4},{14,6},{9,1},{11,3},{13,5},{15,7}} | collective-permute-start | bytes 1327112 | tf_op jit(solution)/shard_map/ppermute | solution.py:92
  595.8 4.1 collective-permute-start.69
  600.0 4.1 collective-permute-start.70
  604.2 5.2 collective-permute-start.71
  609.4 6.2 collective-permute-start.72
  615.6 22.7 %collective-permute-start.73 = (bf16[288,768]{1,0:T(8,128)(2,1)S(1)}, bf16[288,768]{1,0:T(8,128)(2,1)S(1)}, u32[]{:S(2)}, u32[]{:S(2)}) collective-permute-start(bf16[288,768]{1,0:T(8,128)(2,1)S(1)} %get-tuple-element.66), channel_id=1, source_target_pairs={{0,1},{1,0},{2,3},{3,2},{4,5},{5,4},{6,7},{7,6},{8,9},{9,8},{10,11... | collective-permute-start | bytes 1327112 | tf_op jit(solution)/shard_map/ppermute | solution.py:46
  631.7 4.5 collective-permute-start.67
  (90 other events, 914.6 us)
